TPU v7x, 512 devices: a whole 4x4x16 slice. The times are simulated.
512 devices in a mesh: leaf: 16 (over z), row: 8 (over x, core), col: 4 (over y).
Axes of the slice: x: 4, y: 4, z: 16, core: 2. Of those that a mesh axis runs over, the one named last changes fastest.
Arguments:
- pivot: float32 [16, 1024, 1024], P('leaf', 'row', 'col'), as said below
- border: float32 [16, 3072, 1024], P('leaf', 'row', 'col'), may hold values from -0.065625 to 0.065625
- update: float32 [16, 3072, 3072], P('leaf', 'row', 'col'), as said below
- child_map: int32 [16, 3072], replicated, may hold values from 0 to 4607, as said below
- parent_diag: float32 [16, 2304], P('leaf', 'row'), may hold values from 0.5 to 4
Outputs:
- factor_pivot: float32 [16, 1024, 1024], P('leaf', 'row', 'col')
- factor_border: float32 [16, 3072, 1024], P('leaf', 'row', 'col')
- parent_front: float32 [16, 2304, 4608], P('leaf', 'row', 'col')
Inputs may be any that keep to these rules, and one draw needn't show every extreme that they name: Each row child_map[l] is increasing with distinct entries, and its i-th block of 384 entries lies among parent rows i * 576 to (i+1) * 576 - 1. Each pivot[l] is symmetric positive definite. Each update[l] is symmetric.
All inputs are finite; a program needn't handle non-finite values.
Results may differ from a plain program's by a relative error of at most 0.00007.
Values sent between devices are 32-bit elements; how exact they have to be, the bound alone decides.
No kernel may reach another device: no remote copies, remote signals or barrier semaphores. Data moves between devices by JAX's collectives and lax.ppermute only.
A program may use at most 128 MiB of HBM per device.

v0:
```python
import jax
import jax.numpy as jnp
from jax import lax
from jax.sharding import PartitionSpec as P


def spread(value, axis, source):
    kept = jnp.where(lax.axis_index(axis) == source, value, 0).astype(value.dtype)
    return lax.psum(kept, axis)


def swapped(value, axis, stride):
    mask = 2**stride
    pairs = [(source, source ^ mask) for source in range(lax.axis_size(axis))]
    return lax.ppermute(value, axis, pairs)


def place_block(block, rows_to, cols_to, out_rows, out_cols):
    count_rows, count_cols = block.shape
    inverse_cols = (
        jnp.full((out_cols + 1,), count_cols, jnp.int32)
        .at[cols_to]
        .set(jnp.arange(count_cols, dtype=jnp.int32))[:out_cols]
    )
    padded = jnp.concatenate([block, jnp.zeros((count_rows, 1), block.dtype)], axis=1)
    widened = jnp.take(padded, inverse_cols, axis=1)
    inverse_rows = (
        jnp.full((out_rows + 1,), count_rows, jnp.int32)
        .at[rows_to]
        .set(jnp.arange(count_rows, dtype=jnp.int32))[:out_rows]
    )
    padded = jnp.concatenate([widened, jnp.zeros((1, out_cols), block.dtype)], axis=0)
    return jnp.take(padded, inverse_rows, axis=0)


def fetch_columns(factor_rows, nrow, ncol, col_index):
    pieces = max(1, nrow // ncol)
    first = col_index * nrow // ncol
    collected = []
    for step in range(pieces):
        collected.append(spread(factor_rows, "row", first + step))
    joined = jnp.concatenate(collected, axis=0)
    return joined


def on_device(pivot, border, update, child_map, parent_diag):
    nrow = lax.axis_size("row")
    ncol = lax.axis_size("col")
    row_index = lax.axis_index("row")
    col_index = lax.axis_index("col")
    leaf_index = lax.axis_index("leaf")
    piece = pivot[0]
    piece_rows, piece_cols = piece.shape
    stacked = lax.all_gather(piece[None], ("row", "col"), axis=0, tiled=True)
    whole = (
        stacked.reshape(nrow, ncol, piece_rows, piece_cols)
        .transpose(0, 2, 1, 3)
        .reshape(nrow * piece_rows, ncol * piece_cols)
    )
    lower = jnp.linalg.cholesky(whole)
    bord = border[0]
    rows_local = bord.shape[0]
    full_rows = lax.all_gather(bord, "col", axis=1, tiled=True)
    factor_rows = lax.linalg.triangular_solve(
        lower, full_rows, left_side=False, lower=True, transpose_a=True
    )
    pivot_out = lax.dynamic_slice(
        lower, (row_index * piece_rows, col_index * piece_cols), (piece_rows, piece_cols)
    )
    border_out = lax.dynamic_slice_in_dim(factor_rows, col_index * piece_cols, piece_cols, 1)
    trailing = update[0]
    cols_local = trailing.shape[1]
    column_rows = fetch_columns(factor_rows, nrow, ncol, col_index)
    product = lax.dot_general(
        factor_rows,
        column_rows,
        (((1,), (1,)), ((), ())),
        precision=lax.Precision.HIGHEST,
        preferred_element_type=jnp.float32,
    )
    schur = trailing - product
    half_rows = parent_diag.shape[1]
    block_rows = 2 * half_rows
    parent_cols = block_rows * nrow // ncol
    side = leaf_index % 2
    total_cols = child_map.shape[1]
    own_map = lax.dynamic_slice(child_map, (leaf_index, 0), (1, total_cols))[0]
    rows_to = (
        lax.dynamic_slice_in_dim(own_map, row_index * rows_local, rows_local)
        - row_index * block_rows
    )
    cols_to = (
        lax.dynamic_slice_in_dim(own_map, col_index * cols_local, cols_local)
        - col_index * parent_cols
    )
    own_block = place_block(schur, rows_to, cols_to, block_rows, parent_cols)
    mine = lax.dynamic_slice_in_dim(own_block, side * half_rows, half_rows, 0)
    other = lax.dynamic_slice_in_dim(own_block, (1 - side) * half_rows, half_rows, 0)
    received = swapped(other, "leaf", 0)
    assembled = mine + received
    global_rows = row_index * block_rows + side * half_rows + jnp.arange(half_rows, dtype=jnp.int32)
    global_cols = col_index * parent_cols + jnp.arange(parent_cols, dtype=jnp.int32)
    diagonal = jnp.where(global_rows[:, None] == global_cols[None, :], parent_diag[0][:, None], 0.0)
    parent_out = assembled + diagonal
    return (pivot_out[None], border_out[None], parent_out[None])


def solution(mesh):
    placed = (
        P("leaf", "row", "col"),
        P("leaf", "row", "col"),
        P("leaf", "row", "col"),
        P(),
        P("leaf", "row"),
    )
    return jax.shard_map(
        on_device,
        mesh=mesh,
        in_specs=placed,
        out_specs=(P("leaf", "row", "col"), P("leaf", "row", "col"), P("leaf", "row", "col")),
        check_vma=False,
    )
```

profile of v0, /device:TPU:7, one launch (start us, length us, event | category | flops | bytes accessed | tf_op | source)
XLA Modules:
  0.0 585.5 jit_solution(11778522606644715851)
XLA Ops:
  8.7 68.3 %all-gather.4.cloned.1.call-done = f32[32,128,256]{2,1,0:T(8,128)} async-done(((f32[1,128,256]{2,1,0:T(8,128)}), f32[32,128,256]{2,1,0:T(8,128)}) %all-gather.4.cloned.1.call-update) | async-done | bytes 4194320 | tf_op jit(solution)/shard_map/all_gather | solution.py:54
  77.0 5.3 copy.17
  82.3 5.2 copy.28
  87.4 5.3 copy.18
  92.8 5.2 fusion
  99.9 11.7 %cholesky.223 = f32[128,128]{1,0:T(8,128)S(1)} custom-call(f32[128,128]{1,0:T(8,128)S(1)} %cholesky.580), custom_call_target="Cholesky" | custom-call | tf_op jit(solution)/shard_map/jit(cholesky)/cholesky | solution.py:60
  114.1 9.8 %custom-call.62 = f32[1,128,128]{1,2,0:T(8,128)S(1)} custom-call(f32[1,128,128]{2,1,0:T(8,128)S(1)} %get-tuple-element.73), custom_call_target="InvertDiagBlocksLowerTriangular" | custom-call | tf_op jit(solution)/shard_map/jit(cholesky)/cholesky | solution.py:60
  127.8 12.0 %cholesky.244 = f32[128,128]{1,0:T(8,128)S(1)} custom-call(f32[128,128]{1,0:T(8,128)S(1)} %cholesky.584), custom_call_target="Cholesky" | custom-call | tf_op jit(solution)/shard_map/jit(cholesky)/cholesky | solution.py:60
  140.5 9.8 %custom-call.63 = f32[1,128,128]{1,2,0:T(8,128)S(1)} custom-call(f32[1,128,128]{2,1,0:T(8,128)S(1)} %get-tuple-element.70), custom_call_target="InvertDiagBlocksLowerTriangular" | custom-call | tf_op jit(solution)/shard_map/jit(cholesky)/cholesky | solution.py:60
  153.7 11.7 %cholesky.468 = f32[128,128]{1,0:T(8,128)S(1)} custom-call(f32[128,128]{1,0:T(8,128)S(1)} %cholesky.589), custom_call_target="Cholesky" | custom-call | tf_op jit(solution)/shard_map/jit(cholesky)/cholesky | solution.py:60
  166.1 9.8 %custom-call.64 = f32[1,128,128]{1,2,0:T(8,128)S(1)} custom-call(f32[1,128,128]{2,1,0:T(8,128)S(1)} %get-tuple-element.67), custom_call_target="InvertDiagBlocksLowerTriangular" | custom-call | tf_op jit(solution)/shard_map/jit(cholesky)/cholesky | solution.py:60
  179.4 11.9 %cholesky.487 = f32[128,128]{1,0:T(8,128)S(1)} custom-call(f32[128,128]{1,0:T(8,128)S(1)} %cholesky.594), custom_call_target="Cholesky" | custom-call | tf_op jit(solution)/shard_map/jit(cholesky)/cholesky | solution.py:60
  191.9 9.8 %custom-call.65 = f32[1,128,128]{1,2,0:T(8,128)S(1)} custom-call(f32[1,128,128]{2,1,0:T(8,128)S(1)} %get-tuple-element.64), custom_call_target="InvertDiagBlocksLowerTriangular" | custom-call | tf_op jit(solution)/shard_map/jit(cholesky)/cholesky | solution.py:60
  205.2 11.7 %cholesky.506 = f32[128,128]{1,0:T(8,128)S(1)} custom-call(f32[128,128]{1,0:T(8,128)S(1)} %cholesky.599), custom_call_target="Cholesky" | custom-call | tf_op jit(solution)/shard_map/jit(cholesky)/cholesky | solution.py:60
  217.6 10.0 %custom-call.66 = f32[1,128,128]{1,2,0:T(8,128)S(1)} custom-call(f32[1,128,128]{2,1,0:T(8,128)S(1)} %get-tuple-element.61), custom_call_target="InvertDiagBlocksLowerTriangular" | custom-call | tf_op jit(solution)/shard_map/jit(cholesky)/cholesky | solution.py:60
  230.9 11.7 %cholesky.526 = f32[128,128]{1,0:T(8,128)S(1)} custom-call(f32[128,128]{1,0:T(8,128)S(1)} %cholesky.604), custom_call_target="Cholesky" | custom-call | tf_op jit(solution)/shard_map/jit(cholesky)/cholesky | solution.py:60
  243.2 9.8 %custom-call.67 = f32[1,128,128]{1,2,0:T(8,128)S(1)} custom-call(f32[1,128,128]{2,1,0:T(8,128)S(1)} %get-tuple-element.58), custom_call_target="InvertDiagBlocksLowerTriangular" | custom-call | tf_op jit(solution)/shard_map/jit(cholesky)/cholesky | solution.py:60
  256.1 12.1 %cholesky.546 = f32[128,128]{1,0:T(8,128)S(1)} custom-call(f32[128,128]{1,0:T(8,128)S(1)} %cholesky.609), custom_call_target="Cholesky" | custom-call | tf_op jit(solution)/shard_map/jit(cholesky)/cholesky | solution.py:60
  268.8 9.8 %custom-call.68 = f32[1,128,128]{1,2,0:T(8,128)S(1)} custom-call(f32[1,128,128]{2,1,0:T(8,128)S(1)} %get-tuple-element.55), custom_call_target="InvertDiagBlocksLowerTriangular" | custom-call | tf_op jit(solution)/shard_map/jit(cholesky)/cholesky | solution.py:60
  281.2 11.7 %cholesky.564 = f32[128,128]{1,0:T(8,128)S(1)} custom-call(f32[128,128]{1,0:T(8,128)S(1)} %convolution_subtract_fusion.13), custom_call_target="Cholesky" | custom-call | tf_op jit(solution)/shard_map/jit(cholesky)/cholesky | solution.py:60
  303.3 6.6 %fusion.1 = (f32[1024,1024]{1,0:T(8,128)}, f32[1024,1024]{1,0:T(8,128)}) fusion(f32[1024,1024]{1,0:T(8,128)} %get-tuple-element.53, pred[]{:T(512)S(6)} %cholesky.579), kind=kLoop, calls=%fused_computation.11 | loop fusion | flops 4194304 | bytes 12582913 | tf_op jit(solution)/shard_map/triangular_solve | solution.py:64
  309.9 23.2 %while.1 = (s32[]{:T(128)}, f32[1024,1024]{1,0:T(8,128)}, s32[8,2]{0,1:T(2,128)S(1)}, f32[8,128,128]{2,1,0:T(8,128)S(1)}, s32[]{:T(128)}) while((s32[]{:T(128)}, f32[1024,1024]{1,0:T(8,128)}, s32[8,2]{0,1:T(2,128)S(1)}, f32[8,128,128]{2,1,0:T(8,128)S(1)}, s32[]{:T(128)}) %tuple.63), condition=%wide.while_cond, body=%wide.while_body.sunk | while | flops 2 | bytes 131189 | solution.py:64
  333.1 78.8 %custom-call.69 = f32[8,128,128]{1,2,0:T(8,128)S(1)} custom-call(f32[8,128,128]{2,1,0:T(8,128)S(1)} %get-tuple-element.10), custom_call_target="InvertDiagBlocksLowerTriangular" | custom-call | tf_op jit(solution)/shard_map/triangular_solve | solution.py:64
  425.9 3.0 convolution_subtract_fusion.5
  429.3 3.4 convolution_subtract_fusion.4
  436.2 3.4 scatter_custom_fusion.1
  443.5 75.2 %all-reduce.6.cloned.1.call-done = (f32[384,1024]{0,1:T(8,128)}, f32[384,1024]{0,1:T(8,128)}) async-done(((f32[384,1024]{0,1:T(8,128)}, f32[384,1024]{0,1:T(8,128)}), (f32[384,1024]{0,1:T(8,128)}, f32[384,1024]{0,1:T(8,128)})) %all-reduce.6.cloned.1.call-update) | async-done | bytes 3145744 | tf_op jit(solution)/shard_map/psum | solution.py:9
  518.7 6.3 %fusion.6 = f32[384,768]{1,0:T(8,128)S(1)} fusion(f32[384,1024]{0,1:T(8,128)S(1)} %convolution_dynamic-update-slice_fusion.3, f32[384,1024]{0,1:T(8,128)} %get-tuple-element.19, f32[384,1024]{0,1:T(8,128)} %get-tuple-element.20, f32[1,384,768]{2,1,0:T(8,128)} %param.7), kind=kOutput, calls=%fused_computation.17 | convolution fusion | flops 3624960000 | bytes 7077888 | tf_op jit(solution)/shard_map/dot_general | solution.py:74
  527.7 3.5 gather_fusion
  537.1 3.6 gather_fusion.1
  543.8 3.2 collective-permute-start
  550.6 25.5 %collective-permute-done = f32[288,1152]{1,0:T(8,128)} collective-permute-done((f32[288,1152]{1,0:T(8,128)}, f32[288,1152]{1,0:T(8,128)}, u32[]{:S(2)}, u32[]{:S(2)}) %collective-permute-start) | collective-permute-done | bytes 1327136 | tf_op jit(solution)/shard_map/ppermute | solution.py:15
  (118 shorter events, 100.8 us)
Async XLA Ops:
  7.2 69.9 %all-gather.4.cloned.1.call-start = ((), (), s32[]{:S(2)}) async-start(), calls=%async_computation | async-start | bytes 4325376 | tf_op jit(solution)/shard_map/all_gather | solution.py:54
  7.9 404.0 %all-gather.6.cloned.1.call-start = ((), (), s32[]{:S(2)}) async-start(), calls=%async_computation.1 | async-start | bytes 1966080 | tf_op jit(solution)/shard_map/all_gather | solution.py:63
  8.6 510.1 %all-reduce.6.cloned.1.call-start = ((), (), s32[]{:S(2)}) async-start(), calls=%async_computation.2 | async-start | bytes 6291456 | tf_op jit(solution)/shard_map/psum | solution.py:9
  97.9 1.9 copy-start
  411.9 3.4 copy-start.2
  433.3 85.4 %copy-start.1 = (f32[384,1024]{0,1:T(8,128)}, f32[384,1024]{0,1:T(8,128)S(1)}, u32[]{:S(2)}) copy-start(f32[384,1024]{0,1:T(8,128)S(1)} %convolution_dynamic-update-slice_fusion.3) | copy-start | bytes 4718596
  542.6 4.4 copy-start.3
  543.8 32.2 %collective-permute-start = (f32[288,1152]{1,0:T(8,128)}, f32[288,1152]{1,0:T(8,128)}, u32[]{:S(2)}, u32[]{:S(2)}) collective-permute-start(f32[288,1152]{1,0:T(8,128)} %constant_dynamic-slice_fusion.1), channel_id=1, source_target_pairs={{0,32},{32,0},{64,96},{96,64},{128,160},{160,128},{192,224},{224,1... | collective-permute-start | bytes 3981320 | tf_op jit(solution)/shard_map/ppermute | solution.py:15
Sparse Core Ops, SparseCore 0:
  11.1 65.8 all-gather.3
  79.1 33.6 all-gather.5
  435.5 83.1 all-reduce.5
where the time goes:
time: 597 us; the launch traced here: 586 us
  other arithmetic  273 us (46%)
  waiting for transfers between devices  170 us (28%)
  local copies, waits for them, and re-layouts  68.5 us (11%)
  matrix products  50.7 us (8%)
  between operations  19.8 us (3%)
    another operation x30, other arithmetic, on_device(): lower = jnp.linalg.cholesky(whole)  173 us
    another operation x3, other arithmetic, on_device(): lax.linalg.triangular_solve(lower, full_rows, left_side=False, lower=True...  85.4 us
    psum x1, waiting for transfers between devices, spread(): return lax.psum(kept, axis)  75.2 us
    all_gather x1, waiting for transfers between devices, on_device(): stacked = lax.all_gather(piece[None], ('row', 'col'), axis=0, tiled=True)  68.3 us
    ppermute x1, waiting for transfers between devices, swapped(): return lax.ppermute(value, axis, pairs)  25.5 us
    another operation x14, matrix products, on_device(): lower = jnp.linalg.cholesky(whole)  23.1 us
    another operation x24, local copies, waits for them, and re-layouts  23 us
    another operation x15, matrix products, on_device(): lax.linalg.triangular_solve(lower, full_rows, left_side=False, lower=True...  21.3 us
  transfers between devices with their start and end apart: 4, of which 3 were waited for; matrix products, arithmetic and copies ran while one was open for 58% of the time, Pallas kernels for 0%

commit v1 on v0

v1 whole, which is shorter than its diff:
```python
import jax
import jax.numpy as jnp
from jax import lax
from jax.experimental import pallas as pl
from jax.experimental.pallas import tpu as pltpu
from jax.sharding import PartitionSpec as P

HI = lax.Precision.HIGHEST
F32 = jnp.float32
BF16 = jnp.bfloat16
B = 128
SB = 32
H = 64
PAYLOAD = 160
VMEM = pl.BlockSpec(memory_space=pltpu.VMEM)
SMEM = pl.BlockSpec(memory_space=pltpu.SMEM)


def dot_tn(a, b, precision=HI):
    return lax.dot_general(a, b, (((0,), (0,)), ((), ())), precision=precision, preferred_element_type=F32)


def dot_nn(a, b, precision=HI):
    return lax.dot_general(a, b, (((1,), (0,)), ((), ())), precision=precision, preferred_element_type=F32)


def dot_nt(a, b, precision=HI):
    return lax.dot_general(a, b, (((1,), (1,)), ((), ())), precision=precision, preferred_element_type=F32)


def params(flops):
    return dict(
        compiler_params=pltpu.CompilerParams(vmem_limit_bytes=48 * 2**20),
        cost_estimate=pl.CostEstimate(flops=flops, bytes_accessed=2**23, transcendentals=0),
    )


def pack_kernel(idx_ref, p_ref, o_ref):
    row, col = idx_ref[0], idx_ref[1]
    copies = o_ref.shape[0]

    def put(lo, value):
        for q in range(copies):
            o_ref[q, lo : lo + value.shape[0], 0 : value.shape[1]] = value

    for half in range(2):
        block = p_ref[:, half * B : half * B + B]
        other = 2 * col + half

        @pl.when(row <= other)
        def _():
            put(half * H, block[0:H, :])

        @pl.when(row > other)
        def _():
            put(half * H, block[:, H:B].T)

        @pl.when(row == other)
        def _():
            corner = block[H:B, H:B]
            put(2 * H, jnp.concatenate([corner[0:32], corner[32:64]], axis=1))


def unpack(src, parity, u_ref, nrow, ncol):
    for x in range(nrow // 2):
        i = 2 * x + parity
        for y in range(ncol):
            c = x * ncol + y
            for half in range(2):
                o = 2 * y + half
                piece = src[c, half * H : half * H + H, :]
                if i <= o:
                    u_ref[i * B : i * B + H, o * B : o * B + B] = piece
                else:
                    u_ref[o * B + H : o * B + B, i * B : i * B + B] = piece
                if i == o:
                    corner = src[c, 2 * H : 2 * H + 32, :]
                    low = jnp.concatenate([corner[:, 0:H], corner[:, H:B]], axis=0)
                    u_ref[i * B + H : i * B + B, i * B : i * B + B] = jnp.concatenate(
                        [piece[:, H:B].T, low], axis=1
                    )


def spread_row(value, r):
    return jnp.broadcast_to(value[r : r + 1, :], (8, B))


def chain(s_ref, s):
    nb, r0 = SB // 8, s * SB
    rowid = lax.broadcasted_iota(jnp.int32, (8, B), 0)
    blk = [s_ref[r0 + 8 * b : r0 + 8 * b + 8, 0:B] for b in range(nb)]
    c = [
        [
            jnp.broadcast_to(blk[b][:, r0 + i : r0 + i + 1], (8, B)) if b >= i // 8 else None
            for b in range(nb)
        ]
        for i in range(SB)
    ]
    x = [[s_ref[r0 + 8 * b : r0 + 8 * b + 8, B * h : B * h + B] for h in range(2)] for b in range(nb)]
    pivots = [None] * nb
    for j in range(SB):
        bj, rj = j // 8, j % 8
        p = spread_row(c[j][bj], rj)
        inv = 1.0 / p
        pivots[bj] = p if pivots[bj] is None else jnp.where(rowid == rj, p, pivots[bj])
        for i in range(j + 1, SB):
            m = spread_row(c[j][i // 8], i % 8) * inv
            for b in range(i // 8, nb):
                c[i][b] = c[i][b] - c[j][b] * m
        for h in range(2):
            xr = spread_row(x[bj][h], rj) * inv
            for b in range(bj, nb):
                cm = c[j][b] if b > bj else jnp.where(rowid > rj, c[j][b], 0.0)
                x[b][h] = x[b][h] - cm * xr
    out = []
    for b in range(nb):
        q = lax.rsqrt(pivots[b])
        out.append(jnp.concatenate([x[b][0] * q, x[b][1] * q], axis=1))
    return jnp.concatenate(out, axis=0)


def factor_block(s_ref):
    for s in range(B // SB):
        p = chain(s_ref, s)
        s_ref[SB * s : SB * s + SB, :] = p
        lo = SB * (s + 1)
        if lo < B:
            s_ref[lo:, :] = s_ref[lo:, :] - dot_tn(p[:, lo:B], p)


def chol_kernel(idx_ref, mine_ref, other_ref, u_ref, w_ref, l_ref, s_ref):
    row, col, core = idx_ref[0], idx_ref[1], idx_ref[2]
    n = u_ref.shape[0]
    nblk = n // B
    ncol = n // l_ref.shape[1]

    for parity in range(2):

        @pl.when(core == parity)
        def _():
            unpack(mine_ref, parity, u_ref, nblk, ncol)
            unpack(other_ref, 1 - parity, u_ref, nblk, ncol)

    ri = lax.broadcasted_iota(jnp.int32, (B, B), 0)
    ci = lax.broadcasted_iota(jnp.int32, (B, B), 1)
    eye = (ri == ci).astype(F32)

    def body(k, _):
        r0 = pl.multiple_of(k * B, B)
        s_ref[:, 0:B] = u_ref[pl.ds(r0, B), pl.ds(r0, B)]
        s_ref[:, B : 2 * B] = eye
        factor_block(s_ref)
        w = s_ref[:, B : 2 * B]
        for kk in range(nblk):

            @pl.when(k == kk)
            def _():
                lo = (kk + 1) * B
                u_ref[kk * B : lo, kk * B : lo] = jnp.where(ri <= ci, s_ref[:, 0:B], 0.0)
                pair = kk // 2
                if kk % 2 == 0:
                    w_ref[pair, 0:B, 0:B] = w
                    w_ref[pair, 0:B, B : 2 * B] = jnp.zeros((B, B), F32)
                else:
                    w_ref[pair, B : 2 * B, B : 2 * B] = w
                    cross = dot_tn(u_ref[(kk - 1) * B : kk * B, kk * B : lo], w_ref[pair, 0:B, 0:B])
                    w_ref[pair, B : 2 * B, 0:B] = -dot_nn(w, cross)
                if lo < n:
                    panel = dot_nn(w, u_ref[kk * B : lo, lo:])
                    u_ref[kk * B : lo, lo:] = panel
                    t = lo
                    while t < n:
                        m = min(256, n - t)
                        u_ref[t : t + m, t:] = u_ref[t : t + m, t:] - dot_tn(
                            panel[:, t - lo : t - lo + m], panel[:, t - lo :]
                        )
                        t += m

        return 0

    lax.fori_loop(0, nblk, body, 0)
    rows, cols = l_ref.shape
    part = u_ref[pl.ds(pl.multiple_of(col * cols, B), cols), pl.ds(pl.multiple_of(row * rows, B), rows)].T
    rl = lax.broadcasted_iota(jnp.int32, (rows, cols), 0) + row * rows
    cl = lax.broadcasted_iota(jnp.int32, (rows, cols), 1) + col * cols
    l_ref[...] = jnp.where(rl >= cl, part, 0.0)


def split3(value):
    first = value.astype(BF16)
    rest = value - first.astype(F32)
    second = rest.astype(BF16)
    third = (rest - second.astype(F32)).astype(BF16)
    return first, second, third


def pick_rows(onehot, value):
    return sum(dot_nn(onehot, part, None) for part in reversed(split3(value)))


def pick_cols(value, onehot):
    return sum(dot_nt(part, onehot, None) for part in reversed(split3(value)))


def solve_kernel(idx_ref, own_ref, mine_ref, other_ref, u_ref, w_ref, upd_ref, map_ref, fb_ref, keep_ref, send_ref, x_ref):
    row, col, core, side = idx_ref[0], idx_ref[1], idx_ref[2], idx_ref[3]
    ncol, rows, width = own_ref.shape
    n = ncol * width
    for y in range(ncol):
        x_ref[0:rows, y * width : (y + 1) * width] = own_ref[y]
        x_ref[pl.ds((1 + core) * rows, rows), y * width : (y + 1) * width] = mine_ref[y]
        x_ref[pl.ds((2 - core) * rows, rows), y * width : (y + 1) * width] = other_ref[y]
    for k in range(ncol):
        lo, hi = k * width, (k + 1) * width
        f = dot_nt(x_ref[:, lo:hi], w_ref[k])
        x_ref[:, lo:hi] = f
        if hi < n:
            x_ref[:, hi:] = x_ref[:, hi:] - dot_nn(f, u_ref[lo:hi, hi:])
    fb_ref[...] = x_ref[0:rows, pl.ds(pl.multiple_of(col * width, B), width)]
    schur = upd_ref[...] - dot_nt(x_ref[0:rows, :], x_ref[rows:, :])
    half = keep_ref.shape[0]
    place = lax.broadcasted_iota(jnp.int32, (half, rows), 0) + row * 2 * half
    for ref, which in ((send_ref, 1 - side), (keep_ref, side)):
        onehot = (place + which * half == map_ref[...]).astype(F32).astype(BF16)
        ref[...] = pick_rows(onehot, schur)


def widen(value, map_ref, first, base):
    blocks, rows = map_ref.shape
    width = value.shape[1] // blocks
    total = first.shape[1]
    step = total // blocks
    for b in range(blocks):
        lo = b * step // B * B
        hi = -((-(b + 1) * step) // B) * B
        place = lax.broadcasted_iota(jnp.int32, (hi - lo, width), 0) + (lo + base)
        onehot = (place == map_ref[b : b + 1, :]).astype(F32).astype(BF16)
        first[:, lo:hi] = first[:, lo:hi] + pick_cols(value[:, b * width : (b + 1) * width], onehot)


def own_kernel(idx_ref, keep_ref, map_ref, diag_ref, o_ref):
    row, col, side = idx_ref[0], idx_ref[1], idx_ref[3]
    half, total = o_ref.shape
    rid = lax.broadcasted_iota(jnp.int32, (half, total), 0) + (row * 2 + side) * half
    cid = lax.broadcasted_iota(jnp.int32, (half, total), 1) + col * total
    o_ref[...] = jnp.where(rid == cid, diag_ref[...], 0.0)
    widen(keep_ref[...], map_ref, o_ref, col * total)


def add_kernel(idx_ref, got_ref, map_ref, base_ref, o_ref):
    o_ref[...] = base_ref[...]
    widen(got_ref[...], map_ref, o_ref, idx_ref[1] * o_ref.shape[1])


def on_device(pivot, border, update, child_map, parent_diag):
    nrow, ncol = lax.axis_size("row"), lax.axis_size("col")
    row, col, leaf = lax.axis_index("row"), lax.axis_index("col"), lax.axis_index("leaf")
    nx = nrow // 2
    core, side = row % 2, leaf % 2
    idx = jnp.stack([row, col, core, side]).astype(jnp.int32)
    piece_rows, piece_cols = pivot.shape[1:]
    n = piece_rows * nrow
    rows, width = border.shape[1:]
    half = parent_diag.shape[1]
    total = 2 * half * nrow // ncol
    upd_cols = update.shape[2]

    chips = nx * ncol
    packed = pl.pallas_call(
        pack_kernel,
        out_shape=jax.ShapeDtypeStruct((chips, PAYLOAD, B), F32),
        in_specs=[SMEM, VMEM],
        out_specs=VMEM,
        **params(10**6),
    )(idx, pivot[0])
    groups = [[(2 * x + c) * ncol + y for x in range(nx) for y in range(ncol)] for c in range(2)]
    mine = lax.all_to_all(packed, ("row", "col"), 0, 0, axis_index_groups=groups, tiled=True)
    swap = [(r, r ^ 1) for r in range(nrow)]
    other = lax.ppermute(mine, "row", swap)

    own_rows = lax.all_gather(border[0], "col", axis=0)
    turn = [((2 * x + c) * ncol + y, (2 * y + c) * ncol + x) for x in range(nx) for c in range(2) for y in range(ncol)]
    turned = lax.ppermute(border[0], ("row", "col"), turn)
    same = [[2 * x + c for x in range(nx)] for c in range(2)]
    col_rows = lax.all_gather(turned, "row", axis=0, axis_index_groups=same)

    upper, inverse, pivot_out = pl.pallas_call(
        chol_kernel,
        out_shape=(
            jax.ShapeDtypeStruct((n, n), F32),
            jax.ShapeDtypeStruct((n // (2 * B), 2 * B, 2 * B), F32),
            jax.ShapeDtypeStruct((piece_rows, piece_cols), F32),
        ),
        in_specs=[SMEM, VMEM, VMEM],
        out_specs=(VMEM, VMEM, VMEM),
        scratch_shapes=[pltpu.VMEM((B, 2 * B), F32)],
        **params(4 * 10**10),
    )(idx, mine, other)
    other_rows = lax.ppermute(col_rows, "row", swap)

    maps = lax.dynamic_slice(child_map, (leaf, row * rows), (1, rows))
    border_out, keep, send = pl.pallas_call(
        solve_kernel,
        out_shape=(
            jax.ShapeDtypeStruct((rows, width), F32),
            jax.ShapeDtypeStruct((half, upd_cols), F32),
            jax.ShapeDtypeStruct((half, upd_cols), F32),
        ),
        in_specs=[SMEM] + [VMEM] * 7,
        out_specs=(VMEM, VMEM, VMEM),
        scratch_shapes=[pltpu.VMEM((3 * rows, n), F32)],
        **params(10**10),
    )(idx, own_rows, col_rows, other_rows, upper, inverse, update[0], maps)

    got = lax.ppermute(send, "leaf", [(s, s ^ 1) for s in range(lax.axis_size("leaf"))])
    blocks = upd_cols // rows

    def col_maps(which):
        return lax.dynamic_slice(child_map, (which, col * upd_cols), (1, upd_cols)).reshape(blocks, rows)

    base = pl.pallas_call(
        own_kernel,
        out_shape=jax.ShapeDtypeStruct((half, total), F32),
        in_specs=[SMEM] + [VMEM] * 3,
        out_specs=VMEM,
        **params(2 * 10**9),
    )(idx, keep, col_maps(leaf), parent_diag.reshape(half, 1))
    parent_out = pl.pallas_call(
        add_kernel,
        out_shape=jax.ShapeDtypeStruct((half, total), F32),
        in_specs=[SMEM] + [VMEM] * 3,
        out_specs=VMEM,
        **params(2 * 10**9),
    )(idx, got, col_maps(leaf ^ 1), base)
    return pivot_out[None], border_out[None], parent_out[None]


def solution(mesh):
    placed = (
        P("leaf", "row", "col"),
        P("leaf", "row", "col"),
        P("leaf", "row", "col"),
        P(),
        P("leaf", "row"),
    )
    return jax.shard_map(
        on_device,
        mesh=mesh,
        in_specs=placed,
        out_specs=(P("leaf", "row", "col"), P("leaf", "row", "col"), P("leaf", "row", "col")),
        check_vma=False,
    )
```

time: 597 us -> 186 us (0.31); the launches traced: 586 us -> 183 us
  other arithmetic: 273 us -> 0.08 us
  waiting for transfers between devices: 170 us -> 66.5 us
  Pallas kernels: 0 us -> 73.5 us
  local copies, waits for them, and re-layouts: 68.5 us -> 8.38 us
  matrix products: 50.7 us -> 0 us
  starting transfers between devices: 3.29 us -> 20.5 us
    another operation x33 -> x1, other arithmetic: 258 us -> 0.08 us  [on_device(): idx = jnp.stack([row, col, core, side]).astype(jnp.int32)]
    psum x1 -> x0, waiting for transfers between devices: 75.2 us -> none  [spread(): return lax.psum(kept, axis)]
    pallas_call x0 -> x5, Pallas kernels: none -> 73.5 us  [the longest x1 42 us: on_device(): pl.pallas_call(chol_kernel, out_shape=(jax.ShapeDtypeStruct((n, n), F32),...]
    another operation x29 -> x0, matrix products: 44.4 us -> none  [the longest x14 23.1 us: on_device(): lower = jnp.linalg.cholesky(whole)]
    all_gather x2, waiting for transfers between devices: 68.3 us -> 27.6 us  [the longest x1 27.6 us: on_device(): col_rows = lax.all_gather(turned, 'row', axis=0, axis_index_groups=same)]
    another operation x33 -> x0, local copies, waits for them, and re-layouts: 25.6 us -> none
    ppermute x1 -> x4, starting transfers between devices: 3.17 us -> 15.2 us  [the longest x1 4.62 us: on_device(): other = lax.ppermute(mine, 'row', swap)]
    reshape x2 -> x3, local copies, waits for them, and re-layouts: 10.6 us -> 0.15 us  [the longest x1 0.14 us: on_device(): parent_diag.reshape(half, 1)]
  transfers between devices with their start and end apart: 4 -> 7, of which waited for: 3 -> 4; matrix products, arithmetic and copies ran while one was open for 58% -> 1% of each run, Pallas kernels for 0% -> 25%
where the time goes in v1:
time: 186 us; the launch traced here: 183 us
  Pallas kernels  73.5 us (40%)
  waiting for transfers between devices  66.5 us (36%)
  starting transfers between devices  20.5 us (11%)
  between operations  14.2 us (8%)
  local copies, waits for them, and re-layouts  8.38 us (5%)
    pallas_call x1, Pallas kernels, on_device(): pl.pallas_call(chol_kernel, out_shape=(jax.ShapeDtypeStruct((n, n), F32),...  42 us
    all_gather x1, waiting for transfers between devices, on_device(): col_rows = lax.all_gather(turned, 'row', axis=0, axis_index_groups=same)  27.6 us
    pallas_call x1, Pallas kernels, on_device(): pl.pallas_call(solve_kernel, out_shape=(jax.ShapeDtypeStruct((rows, width...  24.1 us
    ppermute x1, waiting for transfers between devices, on_device(): lax.ppermute(send, 'leaf', [(s, s ^ 1) for s in range(lax.axis_size('leaf...  16.7 us
    ppermute x1, waiting for transfers between devices, on_device(): turned = lax.ppermute(border[0], ('row', 'col'), turn)  14.5 us
    all_to_all x1, waiting for transfers between devices, on_device(): lax.all_to_all(packed, ('row', 'col'), 0, 0, axis_index_groups=groups, ti...  7.67 us
    unnamed x14, local copies, waits for them, and re-layouts  6.53 us
    all_to_all x1, starting transfers between devices, on_device(): lax.all_to_all(packed, ('row', 'col'), 0, 0, axis_index_groups=groups, ti...  5.22 us
  transfers between devices with their start and end apart: 7, of which 4 were waited for; matrix products, arithmetic and copies ran while one was open for 1% of the time, Pallas kernels for 25%

profile of v1, /device:TPU:7, one launch (start us, length us, event | category | flops | bytes accessed | tf_op | source)
XLA Modules:
  0.0 183.1 jit_solution(8805062989603895525)
XLA Ops:
  7.2 4.6 %collective-permute-start.1 = (f32[384,256]{1,0:T(8,128)}, f32[384,256]{1,0:T(8,128)S(1)}, u32[]{:S(2)}, u32[]{:S(2)}) collective-permute-start(f32[384,256]{1,0:T(8,128)} %bitcast.14), channel_id=1, source_target_pairs={{0,0},{1,8},{2,16},{3,24},{4,4},{5,12},{6,20},{7,28},{8,1},{9,9},{... | collective-permute-start | bytes 1179656 | tf_op jit(solution)/shard_map/ppermute | solution.py:283
  11.7 0.1 pad_add_fusion.idx_ref
  11.8 0.0 copy-start
  11.8 0.9 copy-done
  12.7 2.0 %shard_map.76 = f32[16,160,128]{2,1,0:T(8,128)} custom-call(s32[4]{0:T(128)S(1)} %pad_add_fusion.idx_ref, f32[128,256]{1,0:T(8,128)S(1)} %bitcast.12), custom_call_target="tpu_custom_call" | custom-call | flops 1000000 | bytes 8388608 | tf_op jit(solution)/shard_map/pallas_call | solution.py:269
  14.7 5.2 %all-to-all-start = ((f32[16,160,128]{2,1,0:T(8,128)}), f32[16,160,128]{2,1,0:T(8,128)S(1)}, u32[]{:S(2)}, u32[]{:S(2)}) async-start(f32[16,160,128]{2,1,0:T(8,128)} %shard_map.76), calls=%async_computation | async-start | bytes 2621440 | tf_op jit(solution)/shard_map/all_to_all | solution.py:277
  19.9 0.0 all-gather.6.cloned.1.call-start
  20.0 14.5 %collective-permute-done.1 = f32[384,256]{1,0:T(8,128)S(1)} collective-permute-done((f32[384,256]{1,0:T(8,128)}, f32[384,256]{1,0:T(8,128)S(1)}, u32[]{:S(2)}, u32[]{:S(2)}) %collective-permute-start.1) | collective-permute-done | bytes 393248 | tf_op jit(solution)/shard_map/ppermute | solution.py:283
  34.5 0.7 copy-done.5
  35.3 0.0 all-gather.6.cloned.1.call-update
  35.3 0.0 all-gather.4.cloned.1.call-start
  35.3 7.7 %all-to-all-done.mine_ref = f32[16,160,128]{2,1,0:T(8,128)S(1)} async-done(((f32[16,160,128]{2,1,0:T(8,128)}), f32[16,160,128]{2,1,0:T(8,128)S(1)}, u32[]{:S(2)}, u32[]{:S(2)}) %all-to-all-start) | async-done | bytes 1310752 | tf_op jit(solution)/shard_map/all_to_all | solution.py:277
  43.0 4.6 %collective-permute-start = (f32[16,160,128]{2,1,0:T(8,128)S(1)}, f32[16,160,128]{2,1,0:T(8,128)S(1)}, u32[]{:S(2)}, u32[]{:S(2)}) collective-permute-start(f32[16,160,128]{2,1,0:T(8,128)S(1)} %all-to-all-done.mine_ref), channel_id=1, source_target_pairs={{0,4},{4,0},{8,12},{12,8},{16,20},{20,16},{24,28},{28,24},{1,5},{5... | collective-permute-start | bytes 3932168 | tf_op jit(solution)/shard_map/ppermute | solution.py:279
  47.6 0.0 all-gather.4.cloned.1.call-update
  47.6 0.8 dynamic_slice.9.map_ref
  48.4 27.6 %all-gather.6.cloned.1.call-done = f32[1536,256]{1,0:T(8,128)} async-done(((f32[384,256]{1,0:T(8,128)}), f32[1536,256]{1,0:T(8,128)}) %all-gather.6.cloned.1.call-update) | async-done | bytes 1572880 | tf_op jit(solution)/shard_map/all_gather | solution.py:285
  76.0 2.9 %collective-permute-start.2 = (f32[4,384,256]{2,1,0:T(8,128)}, f32[4,384,256]{2,1,0:T(8,128)}, u32[]{:S(2)}, u32[]{:S(2)}) collective-permute-start(f32[4,384,256]{2,1,0:T(8,128)} %bitcast.16), channel_id=1, source_target_pairs={{0,4},{4,0},{8,12},{12,8},{16,20},{20,16},{24,28},{28,24},{1,5},{5... | collective-permute-start | bytes 4718600 | tf_op jit(solution)/shard_map/ppermute | solution.py:299
  78.9 0.0 collective-permute-done.other_ref
  78.9 42.0 %shard_map.77 = (f32[1024,1024]{1,0:T(8,128)}, f32[4,256,256]{2,1,0:T(8,128)S(1)}, f32[128,256]{1,0:T(8,128)}) custom-call(s32[4]{0:T(128)S(1)} %pad_add_fusion.idx_ref, f32[16,160,128]{2,1,0:T(8,128)S(1)} %all-to-all-done.mine_ref, f32[16,160,128]{2,1,0:T(8,128)S(1)} %collective-permute-done.other_ref), custom_call_target="tpu_custom_call" | custom-call | flops 40000000000 | bytes 8388608 | tf_op jit(solution)/shard_map/pallas_call | solution.py:287
  120.9 1.0 copy-done.3
  121.9 0.0 collective-permute-done.2.other_ref
  121.9 1.4 copy-done.1
  123.3 1.3 copy-done.2
  124.6 1.2 copy-done.4
  125.8 24.1 %shard_map.78 = (f32[384,256]{1,0:T(8,128)}, f32[288,768]{1,0:T(8,128)S(1)}, f32[288,768]{1,0:T(8,128)S(1)}) custom-call(s32[4]{0:T(128)S(1)} %pad_add_fusion.idx_ref, f32[4,384,256]{2,1,0:T(8,128)S(1)} %copy-done.1, f32[4,384,256]{2,1,0:T(8,128)} %bitcast.17, f32[4,384,256]{2,1,0:T(8,128)} %collective-permute-done.2.other_ref, ...), custom_call_target="tpu_custom_call" | custom-call | flops 10000000000 | bytes 8388608 | tf_op jit(solution)/shard_map/pallas_call | solution.py:302
  149.9 3.2 %collective-permute-start.3 = (f32[288,768]{1,0:T(8,128)S(1)}, f32[288,768]{1,0:T(8,128)S(1)}, u32[]{:S(2)}, u32[]{:S(2)}) collective-permute-start(f32[288,768]{1,0:T(8,128)S(1)} %get-tuple-element.13), channel_id=1, source_target_pairs={{0,32},{32,0},{64,96},{96,64},{128,160},{160,128},{192,224},{224,1... | collective-permute-start | bytes 2654216 | tf_op jit(solution)/shard_map/ppermute | solution.py:315
  153.1 0.9 dynamic-slice_reduce_fusion
  154.1 0.0 copy-done.6
  154.1 0.1 copy.9.diag_ref
  154.2 2.2 %shard_map.79.base_ref = f32[288,1152]{1,0:T(8,128)S(1)} custom-call(s32[4]{0:T(128)S(1)} %pad_add_fusion.idx_ref, f32[288,768]{1,0:T(8,128)S(1)} %get-tuple-element.14.keep_ref, s32[2,384]{1,0:T(2,128)S(1)} %reshape.16.map_ref, f32[288,1]{1,0:T(8,128)S(1)} %copy.9.diag_ref), custom_call_target="tpu_custom_call" | custom-call | flops 2000000000 | bytes 8388608 | tf_op jit(solution)/shard_map/pallas_call | solution.py:321
  156.4 16.7 %collective-permute-done.3.got_ref = f32[288,768]{1,0:T(8,128)S(1)} collective-permute-done((f32[288,768]{1,0:T(8,128)S(1)}, f32[288,768]{1,0:T(8,128)S(1)}, u32[]{:S(2)}, u32[]{:S(2)}) %collective-permute-start.3) | collective-permute-done | bytes 884768 | tf_op jit(solution)/shard_map/ppermute | solution.py:315
  173.1 3.2 %shard_map.80 = f32[288,1152]{1,0:T(8,128)} custom-call(s32[4]{0:T(128)S(1)} %pad_add_fusion.idx_ref, f32[288,768]{1,0:T(8,128)S(1)} %collective-permute-done.3.got_ref, s32[2,384]{1,0:T(2,128)S(1)} %reshape.15.map_ref, f32[288,1152]{1,0:T(8,128)S(1)} %shard_map.79.base_ref), custom_call_target="tpu_custom_call" | custom-call | flops 2000000000 | bytes 8388608 | tf_op jit(solution)/shard_map/pallas_call | solution.py:328
  (9 shorter events, 0.0 us)
Async XLA Ops:
  7.2 27.3 %collective-permute-start.1 = (f32[384,256]{1,0:T(8,128)}, f32[384,256]{1,0:T(8,128)S(1)}, u32[]{:S(2)}, u32[]{:S(2)}) collective-permute-start(f32[384,256]{1,0:T(8,128)} %bitcast.14), channel_id=1, source_target_pairs={{0,0},{1,8},{2,16},{3,24},{4,4},{5,12},{6,20},{7,28},{8,1},{9,9},{... | collective-permute-start | bytes 1179656 | tf_op jit(solution)/shard_map/ppermute | solution.py:283
  11.8 0.9 copy-start
  14.7 28.3 %all-to-all-start = ((f32[16,160,128]{2,1,0:T(8,128)}), f32[16,160,128]{2,1,0:T(8,128)S(1)}, u32[]{:S(2)}, u32[]{:S(2)}) async-start(f32[16,160,128]{2,1,0:T(8,128)} %shard_map.76), calls=%async_computation | async-start | bytes 2621440 | tf_op jit(solution)/shard_map/all_to_all | solution.py:277
  19.9 56.1 %all-gather.6.cloned.1.call-start = ((), (), s32[]{:S(2)}) async-start(), calls=%async_computation.2 | async-start | bytes 1966080 | tf_op jit(solution)/shard_map/all_gather | solution.py:285
  34.5 0.7 copy-start.5
  35.3 86.6 %all-gather.4.cloned.1.call-start = ((), (), s32[]{:S(2)}) async-start(), calls=%async_computation.1 | async-start | bytes 1966080 | tf_op jit(solution)/shard_map/all_gather | solution.py:281
  43.0 35.9 %collective-permute-start = (f32[16,160,128]{2,1,0:T(8,128)S(1)}, f32[16,160,128]{2,1,0:T(8,128)S(1)}, u32[]{:S(2)}, u32[]{:S(2)}) collective-permute-start(f32[16,160,128]{2,1,0:T(8,128)S(1)} %all-to-all-done.mine_ref), channel_id=1, source_target_pairs={{0,4},{4,0},{8,12},{12,8},{16,20},{20,16},{24,28},{28,24},{1,5},{5... | collective-permute-start | bytes 3932168 | tf_op jit(solution)/shard_map/ppermute | solution.py:279
  76.0 45.9 %collective-permute-start.2 = (f32[4,384,256]{2,1,0:T(8,128)}, f32[4,384,256]{2,1,0:T(8,128)}, u32[]{:S(2)}, u32[]{:S(2)}) collective-permute-start(f32[4,384,256]{2,1,0:T(8,128)} %bitcast.16), channel_id=1, source_target_pairs={{0,4},{4,0},{8,12},{12,8},{16,20},{20,16},{24,28},{28,24},{1,5},{5... | collective-permute-start | bytes 4718600 | tf_op jit(solution)/shard_map/ppermute | solution.py:299
  120.9 1.0 copy-start.3
  121.9 1.4 copy-start.1
  123.3 1.3 copy-start.2
  124.6 1.2 copy-start.4
  125.8 28.3 %copy-start.6 = (f32[1,288]{1,0:T(1,128)S(1)}, f32[1,288]{1,0:T(1,128)}, u32[]{:S(2)}) copy-start(f32[1,288]{1,0:T(1,128)} %param.9) | copy-start | bytes 3460
  149.9 23.2 %collective-permute-start.3 = (f32[288,768]{1,0:T(8,128)S(1)}, f32[288,768]{1,0:T(8,128)S(1)}, u32[]{:S(2)}, u32[]{:S(2)}) collective-permute-start(f32[288,768]{1,0:T(8,128)S(1)} %get-tuple-element.13), channel_id=1, source_target_pairs={{0,32},{32,0},{64,96},{96,64},{128,160},{160,128},{192,224},{224,1... | collective-permute-start | bytes 2654216 | tf_op jit(solution)/shard_map/ppermute | solution.py:315
Sparse Core Ops, SparseCore 0:
  35.4 40.5 all-gather.5
  78.1 35.8 all-gather.3

commit v2 on v1

--- a/solution.py
+++ b/solution.py
@@ -13,6 +13,7 @@
 H = 64
 PAYLOAD = 160
 VMEM = pl.BlockSpec(memory_space=pltpu.VMEM)
+HBM = pl.BlockSpec(memory_space=pltpu.HBM)
 SMEM = pl.BlockSpec(memory_space=pltpu.SMEM)
 
 
@@ -28,9 +29,9 @@
     return lax.dot_general(a, b, (((1,), (1,)), ((), ())), precision=precision, preferred_element_type=F32)
 
 
-def params(flops):
+def params(flops, mib=60):
     return dict(
-        compiler_params=pltpu.CompilerParams(vmem_limit_bytes=48 * 2**20),
+        compiler_params=pltpu.CompilerParams(vmem_limit_bytes=mib * 2**20),
         cost_estimate=pl.CostEstimate(flops=flops, bytes_accessed=2**23, transcendentals=0),
     )
 
@@ -128,19 +129,8 @@
             s_ref[lo:, :] = s_ref[lo:, :] - dot_tn(p[:, lo:B], p)
 
 
-def chol_kernel(idx_ref, mine_ref, other_ref, u_ref, w_ref, l_ref, s_ref):
-    row, col, core = idx_ref[0], idx_ref[1], idx_ref[2]
-    n = u_ref.shape[0]
-    nblk = n // B
-    ncol = n // l_ref.shape[1]
-
-    for parity in range(2):
-
-        @pl.when(core == parity)
-        def _():
-            unpack(mine_ref, parity, u_ref, nblk, ncol)
-            unpack(other_ref, 1 - parity, u_ref, nblk, ncol)
-
+def chol_steps(u_ref, w_ref, s_ref, steps):
+    n = u_ref.shape[1]
     ri = lax.broadcasted_iota(jnp.int32, (B, B), 0)
     ci = lax.broadcasted_iota(jnp.int32, (B, B), 1)
     eye = (ri == ci).astype(F32)
@@ -151,7 +141,7 @@
         s_ref[:, B : 2 * B] = eye
         factor_block(s_ref)
         w = s_ref[:, B : 2 * B]
-        for kk in range(nblk):
+        for kk in range(steps):
 
             @pl.when(k == kk)
             def _():
@@ -178,12 +168,65 @@
 
         return 0
 
-    lax.fori_loop(0, nblk, body, 0)
+    lax.fori_loop(0, steps, body, 0)
+
+
+def lower_block(u_ref, l_ref, row, first_col, col):
     rows, cols = l_ref.shape
-    part = u_ref[pl.ds(pl.multiple_of(col * cols, B), cols), pl.ds(pl.multiple_of(row * rows, B), rows)].T
+    start = pl.multiple_of((col - first_col) * cols, B)
+    part = u_ref[pl.ds(start, cols), pl.ds(pl.multiple_of(row * rows - first_col * cols, B), rows)].T
     rl = lax.broadcasted_iota(jnp.int32, (rows, cols), 0) + row * rows
     cl = lax.broadcasted_iota(jnp.int32, (rows, cols), 1) + col * cols
     l_ref[...] = jnp.where(rl >= cl, part, 0.0)
+
+
+def copy_all(sources, targets, sems):
+    copies = [pltpu.make_async_copy(s, t, sems.at[i]) for i, (s, t) in enumerate(zip(sources, targets))]
+    for copy in copies:
+        copy.start()
+    return copies
+
+
+def chol_first(idx_ref, mine_ref, other_ref, top_ref, rest_ref, w_ref, l_ref, u_ref, v_ref, s_ref, sems):
+    row, col, core = idx_ref[0], idx_ref[1], idx_ref[2]
+    nblk = u_ref.shape[0] // B
+    ncol = mine_ref.shape[0] // (nblk // 2)
+    for parity in range(2):
+
+        @pl.when(core == parity)
+        def _():
+            unpack(mine_ref, parity, u_ref, nblk, ncol)
+            unpack(other_ref, 1 - parity, u_ref, nblk, ncol)
+
+    done = top_ref.shape[0]
+    left = u_ref.shape[0] - done
+    chol_steps(u_ref, v_ref, s_ref, done // B)
+    sources = (u_ref.at[pl.ds(done, left), pl.ds(done, left)], u_ref.at[pl.ds(0, done)], v_ref)
+    copies = copy_all(sources, (rest_ref, top_ref, w_ref), sems)
+
+    @pl.when(col < w_ref.shape[0])
+    def _():
+        lower_block(u_ref, l_ref, row, 0, col)
+
+    for copy in copies:
+        copy.wait()
+
+
+def chol_last(idx_ref, rest_ref, before_ref, last_ref, w_ref, l_ref, u_ref, v_ref, s_ref, sems):
+    row, col, ncol = idx_ref[0], idx_ref[1], idx_ref[4]
+    copy_all((rest_ref,), (u_ref,), sems)[0].wait()
+    chol_steps(u_ref, v_ref, s_ref, u_ref.shape[0] // B)
+    copies = copy_all((u_ref, v_ref), (last_ref, w_ref), sems)
+    rows, cols = l_ref.shape
+    first_col = ncol - u_ref.shape[0] // cols
+    l_ref[...] = jnp.where(col < first_col, before_ref[...], 0.0)
+
+    @pl.when((col >= first_col) & (row * rows >= first_col * cols))
+    def _():
+        lower_block(u_ref, l_ref, row, first_col, col)
+
+    for copy in copies:
+        copy.wait()
 
 
 def split3(value):
@@ -194,35 +237,88 @@
     return first, second, third
 
 
-def pick_rows(onehot, value):
-    return sum(dot_nn(onehot, part, None) for part in reversed(split3(value)))
-
-
-def pick_cols(value, onehot):
-    return sum(dot_nt(part, onehot, None) for part in reversed(split3(value)))
-
-
-def solve_kernel(idx_ref, own_ref, mine_ref, other_ref, u_ref, w_ref, upd_ref, map_ref, fb_ref, keep_ref, send_ref, x_ref):
+def pick_rows(onehot, parts):
+    return sum(dot_nn(onehot, part, None) for part in reversed(parts))
+
+
+def pick_cols(parts, onehot):
+    return sum(dot_nt(part, onehot, None) for part in reversed(parts))
+
+
+def split2(value):
+    first = value.astype(BF16)
+    return first, (value - first.astype(F32)).astype(BF16)
+
+
+def dot3(dot, a, b):
+    return dot(a[0], b[1], None) + dot(a[1], b[0], None) + dot(a[0], b[0], None)
+
+
+def solve_kernel(
+    idx_ref, own_ref, mine_ref, other_ref, top_ref, last_ref, w0_ref, w1_ref, upd_ref, map_ref,
+    fb_ref, schur_ref, send_ref,
+    x_ref, u0_ref, u1_ref, v_ref, fh_ref, fl_ref, t_ref, o_ref, sem, sems,
+):
     row, col, core, side = idx_ref[0], idx_ref[1], idx_ref[2], idx_ref[3]
     ncol, rows, width = own_ref.shape
-    n = ncol * width
-    for y in range(ncol):
-        x_ref[0:rows, y * width : (y + 1) * width] = own_ref[y]
-        x_ref[pl.ds((1 + core) * rows, rows), y * width : (y + 1) * width] = mine_ref[y]
-        x_ref[pl.ds((2 - core) * rows, rows), y * width : (y + 1) * width] = other_ref[y]
+    early = w0_ref.shape[0]
+
+    def load(y):
+        cols = pl.ds(y * width, width)
+        found = [pltpu.make_async_copy(own_ref.at[y], x_ref.at[pl.ds(0, rows), cols], sem.at[y, 0])]
+        for c, ref in ((core, mine_ref), (1 - core, other_ref)):
+            target = pl.ds(pl.multiple_of((1 + c) * rows, B), rows)
+            which = 1 if ref is mine_ref else 2
+            found.append(pltpu.make_async_copy(ref.at[y], x_ref.at[target, cols], sem.at[y, which]))
+        if y < early:
+            tall = pl.ds(y * width, width)
+            found.append(pltpu.make_async_copy(top_ref.at[tall], u0_ref.at[tall], sem.at[y, 3]))
+            found.append(pltpu.make_async_copy(w0_ref.at[y], v_ref.at[y], sem.at[y, 4]))
+        else:
+            tall = pl.ds((y - early) * width, width)
+            found.append(pltpu.make_async_copy(last_ref.at[tall], u1_ref.at[tall], sem.at[y, 3]))
+            found.append(pltpu.make_async_copy(w1_ref.at[y - early], v_ref.at[y], sem.at[y, 4]))
+        for copy in found:
+            copy.start()
+        return found
+
+    waiting = [load(y) for y in range(ncol)]
+    trailing = pltpu.make_async_copy(upd_ref, t_ref, sems.at[0])
+    trailing.start()
+    cut = u0_ref.shape[0]
     for k in range(ncol):
+        for copy in waiting[k]:
+            copy.wait()
         lo, hi = k * width, (k + 1) * width
-        f = dot_nt(x_ref[:, lo:hi], w_ref[k])
-        x_ref[:, lo:hi] = f
-        if hi < n:
-            x_ref[:, hi:] = x_ref[:, hi:] - dot_nn(f, u_ref[lo:hi, hi:])
-    fb_ref[...] = x_ref[0:rows, pl.ds(pl.multiple_of(col * width, B), width)]
-    schur = upd_ref[...] - dot_nt(x_ref[0:rows, :], x_ref[rows:, :])
-    half = keep_ref.shape[0]
-    place = lax.broadcasted_iota(jnp.int32, (half, rows), 0) + row * 2 * half
-    for ref, which in ((send_ref, 1 - side), (keep_ref, side)):
-        onehot = (place + which * half == map_ref[...]).astype(F32).astype(BF16)
-        ref[...] = pick_rows(onehot, schur)
+        x = x_ref[:, lo:hi]
+        if k > 0:
+            top = min(lo, cut)
+            x = x - dot3(dot_nn, (fh_ref[:, 0:top], fl_ref[:, 0:top]), split2(u0_ref[0:top, lo:hi]))
+            if lo > cut:
+                above = split2(u1_ref[0 : lo - cut, lo - cut : hi - cut])
+                x = x - dot3(dot_nn, (fh_ref[:, cut:lo], fl_ref[:, cut:lo]), above)
+        f = dot3(dot_nt, split2(x), split2(v_ref[k]))
+        fh_ref[:, lo:hi], fl_ref[:, lo:hi] = split2(f)
+
+        @pl.when(col == k)
+        def _():
+            fb_ref[...] = f[0:rows]
+
+    trailing.wait()
+    schur = t_ref[...] - dot3(
+        dot_nt, (fh_ref[0:rows, :], fl_ref[0:rows, :]), (fh_ref[rows:, :], fl_ref[rows:, :])
+    )
+    t_ref[...] = schur
+    out = pltpu.make_async_copy(t_ref, schur_ref, sems.at[1])
+    out.start()
+    half = o_ref.shape[0]
+    place = lax.broadcasted_iota(jnp.int32, (half, rows), 0) + (row * 2 + 1 - side) * half
+    onehot = (place == map_ref[...]).astype(F32).astype(BF16)
+    o_ref[...] = pick_rows(onehot, split3(schur))
+    sent = pltpu.make_async_copy(o_ref, send_ref, sems.at[2])
+    sent.start()
+    out.wait()
+    sent.wait()
 
 
 def widen(value, map_ref, first, base):
@@ -235,16 +331,18 @@
         hi = -((-(b + 1) * step) // B) * B
         place = lax.broadcasted_iota(jnp.int32, (hi - lo, width), 0) + (lo + base)
         onehot = (place == map_ref[b : b + 1, :]).astype(F32).astype(BF16)
-        first[:, lo:hi] = first[:, lo:hi] + pick_cols(value[:, b * width : (b + 1) * width], onehot)
-
-
-def own_kernel(idx_ref, keep_ref, map_ref, diag_ref, o_ref):
+        first[:, lo:hi] = first[:, lo:hi] + pick_cols(split3(value[:, b * width : (b + 1) * width]), onehot)
+
+
+def own_kernel(idx_ref, schur_ref, row_map_ref, map_ref, diag_ref, o_ref):
     row, col, side = idx_ref[0], idx_ref[1], idx_ref[3]
     half, total = o_ref.shape
     rid = lax.broadcasted_iota(jnp.int32, (half, total), 0) + (row * 2 + side) * half
     cid = lax.broadcasted_iota(jnp.int32, (half, total), 1) + col * total
     o_ref[...] = jnp.where(rid == cid, diag_ref[...], 0.0)
-    widen(keep_ref[...], map_ref, o_ref, col * total)
+    place = lax.broadcasted_iota(jnp.int32, (half, schur_ref.shape[0]), 0) + (row * 2 + side) * half
+    onehot = (place == row_map_ref[...]).astype(F32).astype(BF16)
+    widen(pick_rows(onehot, split3(schur_ref[...])), map_ref, o_ref, col * total)
 
 
 def add_kernel(idx_ref, got_ref, map_ref, base_ref, o_ref):
@@ -257,7 +355,7 @@
     row, col, leaf = lax.axis_index("row"), lax.axis_index("col"), lax.axis_index("leaf")
     nx = nrow // 2
     core, side = row % 2, leaf % 2
-    idx = jnp.stack([row, col, core, side]).astype(jnp.int32)
+    idx = jnp.stack([row, col, core, side, jnp.int32(ncol)]).astype(jnp.int32)
     piece_rows, piece_cols = pivot.shape[1:]
     n = piece_rows * nrow
     rows, width = border.shape[1:]
@@ -276,41 +374,82 @@
     groups = [[(2 * x + c) * ncol + y for x in range(nx) for y in range(ncol)] for c in range(2)]
     mine = lax.all_to_all(packed, ("row", "col"), 0, 0, axis_index_groups=groups, tiled=True)
     swap = [(r, r ^ 1) for r in range(nrow)]
-    other = lax.ppermute(mine, "row", swap)
-
-    own_rows = lax.all_gather(border[0], "col", axis=0)
+
     turn = [((2 * x + c) * ncol + y, (2 * y + c) * ncol + x) for x in range(nx) for c in range(2) for y in range(ncol)]
     turned = lax.ppermute(border[0], ("row", "col"), turn)
+    turned, mine = lax.optimization_barrier((turned, mine))
+    other = lax.ppermute(mine, "row", swap)
     same = [[2 * x + c for x in range(nx)] for c in range(2)]
-    col_rows = lax.all_gather(turned, "row", axis=0, axis_index_groups=same)
-
-    upper, inverse, pivot_out = pl.pallas_call(
-        chol_kernel,
+    col_mine = lax.all_to_all(
+        jnp.broadcast_to(turned, (nx, rows, width)), "row", 0, 0, axis_index_groups=same, tiled=True
+    )
+
+    pairs = n // (2 * B)
+    early = 2
+    inv = lambda count: jax.ShapeDtypeStruct((count, 2 * B, 2 * B), F32)
+    done = early * 2 * B
+    block = jax.ShapeDtypeStruct((piece_rows, piece_cols), F32)
+    top, rest, inv0, begun = pl.pallas_call(
+        chol_first,
         out_shape=(
-            jax.ShapeDtypeStruct((n, n), F32),
-            jax.ShapeDtypeStruct((n // (2 * B), 2 * B, 2 * B), F32),
-            jax.ShapeDtypeStruct((piece_rows, piece_cols), F32),
+            jax.ShapeDtypeStruct((done, n), F32),
+            jax.ShapeDtypeStruct((n - done, n - done), F32),
+            inv(early),
+            block,
         ),
         in_specs=[SMEM, VMEM, VMEM],
-        out_specs=(VMEM, VMEM, VMEM),
-        scratch_shapes=[pltpu.VMEM((B, 2 * B), F32)],
-        **params(4 * 10**10),
+        out_specs=(HBM, HBM, HBM, VMEM),
+        scratch_shapes=[
+            pltpu.VMEM((n, n), F32),
+            pltpu.VMEM((early, 2 * B, 2 * B), F32),
+            pltpu.VMEM((B, 2 * B), F32),
+            pltpu.SemaphoreType.DMA((3,)),
+        ],
+        **params(10**10),
     )(idx, mine, other)
-    other_rows = lax.ppermute(col_rows, "row", swap)
+
+    bord, col_mine, inv0 = lax.optimization_barrier((border[0], col_mine, inv0))
+    col_other = lax.ppermute(col_mine, "row", swap)
+    own_rows = lax.all_to_all(jnp.broadcast_to(bord, (ncol, rows, width)), "col", 0, 0, tiled=True)
+
+    last, inv1, pivot_out = pl.pallas_call(
+        chol_last,
+        out_shape=(jax.ShapeDtypeStruct((n - done, n - done), F32), inv(pairs - early), block),
+        in_specs=[SMEM, HBM, VMEM],
+        out_specs=(HBM, HBM, VMEM),
+        scratch_shapes=[
+            pltpu.VMEM((n - done, n - done), F32),
+            pltpu.VMEM((pairs - early, 2 * B, 2 * B), F32),
+            pltpu.VMEM((B, 2 * B), F32),
+            pltpu.SemaphoreType.DMA((2,)),
+        ],
+        **params(3 * 10**10),
+    )(idx, rest, begun)
 
     maps = lax.dynamic_slice(child_map, (leaf, row * rows), (1, rows))
-    border_out, keep, send = pl.pallas_call(
+    border_out, schur, send = pl.pallas_call(
         solve_kernel,
         out_shape=(
             jax.ShapeDtypeStruct((rows, width), F32),
-            jax.ShapeDtypeStruct((half, upd_cols), F32),
+            jax.ShapeDtypeStruct((rows, upd_cols), F32),
             jax.ShapeDtypeStruct((half, upd_cols), F32),
         ),
-        in_specs=[SMEM] + [VMEM] * 7,
-        out_specs=(VMEM, VMEM, VMEM),
-        scratch_shapes=[pltpu.VMEM((3 * rows, n), F32)],
+        in_specs=[SMEM] + [HBM] * 8 + [VMEM],
+        out_specs=(VMEM, HBM, HBM),
+        scratch_shapes=[
+            pltpu.VMEM((3 * rows, n), F32),
+            pltpu.VMEM((done, n), F32),
+            pltpu.VMEM((n - done, n - done), F32),
+            pltpu.VMEM((pairs, 2 * B, 2 * B), F32),
+            pltpu.VMEM((3 * rows, n), BF16),
+            pltpu.VMEM((3 * rows, n), BF16),
+            pltpu.VMEM((rows, upd_cols), F32),
+            pltpu.VMEM((half, upd_cols), F32),
+            pltpu.SemaphoreType.DMA((ncol, 5)),
+            pltpu.SemaphoreType.DMA((3,)),
+        ],
         **params(10**10),
-    )(idx, own_rows, col_rows, other_rows, upper, inverse, update[0], maps)
+    )(idx, own_rows, col_mine, col_other, top, last, inv0, inv1, update[0], maps)
 
     got = lax.ppermute(send, "leaf", [(s, s ^ 1) for s in range(lax.axis_size("leaf"))])
     blocks = upd_cols // rows
@@ -321,16 +460,16 @@
     base = pl.pallas_call(
         own_kernel,
         out_shape=jax.ShapeDtypeStruct((half, total), F32),
-        in_specs=[SMEM] + [VMEM] * 3,
+        in_specs=[SMEM] + [VMEM] * 4,
         out_specs=VMEM,
-        **params(2 * 10**9),
-    )(idx, keep, col_maps(leaf), parent_diag.reshape(half, 1))
+        **params(2 * 10**9, 16),
+    )(idx, schur, maps, col_maps(leaf), parent_diag.reshape(half, 1))
     parent_out = pl.pallas_call(
         add_kernel,
         out_shape=jax.ShapeDtypeStruct((half, total), F32),
         in_specs=[SMEM] + [VMEM] * 3,
         out_specs=VMEM,
-        **params(2 * 10**9),
+        **params(2 * 10**9, 16),
     )(idx, got, col_maps(leaf ^ 1), base)
     return pivot_out[None], border_out[None], parent_out[None]
 

time: 186 us -> 159 us (0.85); the launches traced: 183 us -> 158 us
  waiting for transfers between devices: 66.5 us -> 46.3 us
  between operations: 14.2 us -> 0.86 us
  starting transfers between devices: 20.5 us -> 31.2 us
    all_gather x2 -> x0, waiting for transfers between devices: 27.6 us -> none  [the longest x1 27.6 us: on_device(): col_rows = lax.all_gather(turned, 'row', axis=0, axis_index_groups=same)]
    ppermute x1, waiting for transfers between devices: 14.5 us -> 31.4 us  [on_device(): turned = lax.ppermute(border[0], ('row', 'col'), turn)]
    all_to_all x0 -> x2, starting transfers between devices: none -> 8.29 us  [the longest x1 4.35 us: on_device(): lax.all_to_all(jnp.broadcast_to(bord, (ncol, rows, width)), 'col', 0, 0,...]
    all_to_all x1, waiting for transfers between devices: 7.67 us -> 0.01 us  [on_device(): lax.all_to_all(packed, ('row', 'col'), 0, 0, axis_index_groups=groups, ti...]
    pallas_call x1, Pallas kernels: 24.1 us -> 16.7 us  [on_device(): pl.pallas_call(solve_kernel, out_shape=(jax.ShapeDtypeStruct((rows, width...]
    pallas_call x1 -> x2, Pallas kernels: 42 us -> 47.4 us  [the longest x1 26.2 us: on_device(): pl.pallas_call(chol_first, out_shape=(jax.ShapeDtypeStruct((done, n), F32...]
    unnamed x14 -> x12, local copies, waits for them, and re-layouts: 6.53 us -> 1.29 us
    broadcast_in_dim x0 -> x2, local copies, waits for them, and re-layouts: none -> 2.7 us  [the longest x1 1.41 us: on_device(): jnp.broadcast_to(bord, (ncol, rows, width))]
  transfers between devices with their start and end apart: 7 -> 7, of which waited for: 4 -> 2; matrix products, arithmetic and copies ran while one was open for 1% -> 2% of each run, Pallas kernels for 25% -> 32%
where the time goes in v2:
time: 159 us; the launch traced here: 158 us
  Pallas kernels  72.6 us (46%)
  waiting for transfers between devices  46.3 us (29%)
  starting transfers between devices  31.2 us (20%)
  local copies, waits for them, and re-layouts  7.07 us (4%)
    ppermute x1, waiting for transfers between devices, on_device(): turned = lax.ppermute(border[0], ('row', 'col'), turn)  31.4 us
    pallas_call x1, Pallas kernels, on_device(): pl.pallas_call(chol_first, out_shape=(jax.ShapeDtypeStruct((done, n), F32...  26.2 us
    pallas_call x1, Pallas kernels, on_device(): pl.pallas_call(chol_last, out_shape=(jax.ShapeDtypeStruct((n - done, n -...  21.2 us
    pallas_call x1, Pallas kernels, on_device(): pl.pallas_call(solve_kernel, out_shape=(jax.ShapeDtypeStruct((rows, width...  16.7 us
    ppermute x1, waiting for transfers between devices, on_device(): lax.ppermute(send, 'leaf', [(s, s ^ 1) for s in range(lax.axis_size('leaf...  14.9 us
    all_to_all x1, starting transfers between devices, on_device(): lax.all_to_all(packed, ('row', 'col'), 0, 0, axis_index_groups=groups, ti...  6.94 us
    ppermute x1, starting transfers between devices, on_device(): lax.ppermute(send, 'leaf', [(s, s ^ 1) for s in range(lax.axis_size('leaf...  4.59 us
    ppermute x1, starting transfers between devices, on_device(): other = lax.ppermute(mine, 'row', swap)  4.44 us
  transfers between devices with their start and end apart: 7, of which 2 were waited for; matrix products, arithmetic and copies ran while one was open for 2% of the time, Pallas kernels for 32%

profile of v2, /device:TPU:7, one launch (start us, length us, event | category | flops | bytes accessed | tf_op | source)
XLA Modules:
  0.0 158.0 jit_solution(8012455684131277413)
XLA Ops:
  0.7 0.7 stack.19.idx_ref
  1.3 2.4 %shard_map.76 = f32[16,160,128]{2,1,0:T(8,128)} custom-call(s32[5]{0:T(128)} %stack.19.idx_ref, f32[128,256]{1,0:T(8,128)} %bitcast.13), custom_call_target="tpu_custom_call" | custom-call | flops 1000000 | bytes 8388608 | tf_op jit(solution)/shard_map/pallas_call | solution.py:367
  3.7 6.9 %all-to-all-start = ((f32[16,160,128]{2,1,0:T(8,128)}), f32[16,160,128]{2,1,0:T(8,128)}, u32[]{:S(2)}, u32[]{:S(2)}) async-start(f32[16,160,128]{2,1,0:T(8,128)} %shard_map.76), calls=%async_computation | async-start | bytes 2621440 | tf_op jit(solution)/shard_map/all_to_all | solution.py:375
  10.6 0.0 copy-done.4
  10.6 4.3 %collective-permute-start = (f32[384,256]{1,0:T(8,128)S(1)}, f32[384,256]{1,0:T(8,128)S(1)}, u32[]{:S(2)}, u32[]{:S(2)}) collective-permute-start(f32[384,256]{1,0:T(8,128)S(1)} %bitcast.11), channel_id=1, source_target_pairs={{0,0},{1,8},{2,16},{3,24},{4,4},{5,12},{6,20},{7,28},{8,1},{9,9},{... | collective-permute-start | bytes 1179656 | tf_op jit(solution)/shard_map/ppermute | solution.py:379
  14.9 31.4 %collective-permute-done = f32[384,256]{1,0:T(8,128)S(1)} collective-permute-done((f32[384,256]{1,0:T(8,128)S(1)}, f32[384,256]{1,0:T(8,128)S(1)}, u32[]{:S(2)}, u32[]{:S(2)}) %collective-permute-start) | collective-permute-done | bytes 393248 | tf_op jit(solution)/shard_map/ppermute | solution.py:379
  46.3 0.0 all-to-all-done.mine_ref
  46.3 4.4 %collective-permute-start.1 = (f32[16,160,128]{2,1,0:T(8,128)}, f32[16,160,128]{2,1,0:T(8,128)}, u32[]{:S(2)}, u32[]{:S(2)}) collective-permute-start(f32[16,160,128]{2,1,0:T(8,128)} %all-to-all-done.mine_ref), channel_id=1, source_target_pairs={{0,4},{4,0},{8,12},{12,8},{16,20},{20,16},{24,28},{28,24},{1,5},{5... | collective-permute-start | bytes 3932168 | tf_op jit(solution)/shard_map/ppermute | solution.py:381
  50.8 1.3 broadcast_in_dim.16
  52.1 3.9 %all-to-all-start.1 = ((f32[4,384,256]{2,1,0:T(8,128)}), f32[4,384,256]{2,1,0:T(8,128)S(1)}, u32[]{:S(2)}, u32[]{:S(2)}) async-start(f32[4,384,256]{2,1,0:T(8,128)} %broadcast_in_dim.16), calls=%async_computation.1 | async-start | bytes 3145728 | tf_op jit(solution)/shard_map/all_to_all | solution.py:383
  56.0 1.4 dynamic_slice.9.map_ref.row_map_ref
  57.4 0.0 collective-permute-done.1.other_ref
  57.4 26.2 %shard_map.77 = (f32[512,1024]{1,0:T(8,128)}, f32[512,512]{1,0:T(8,128)}, f32[2,256,256]{2,1,0:T(8,128)}, f32[128,256]{1,0:T(8,128)}) custom-call(s32[5]{0:T(128)} %stack.19.idx_ref, f32[16,160,128]{2,1,0:T(8,128)} %all-to-all-done.mine_ref, f32[16,160,128]{2,1,0:T(8,128)} %collective-permute-done.1.other_ref), custom_call_target="tpu_custom_call" | custom-call | flops 10000000000 | bytes 8388608 | tf_op jit(solution)/shard_map/pallas_call | solution.py:392
  83.5 0.0 all-to-all-done.1.mine_ref
  83.5 0.0 copy-start.3
  83.6 1.4 broadcast_in_dim.17
  85.0 4.3 %all-to-all-start.2 = ((f32[4,384,256]{2,1,0:T(8,128)}), f32[4,384,256]{2,1,0:T(8,128)}, u32[]{:S(2)}, u32[]{:S(2)}) async-start(f32[4,384,256]{2,1,0:T(8,128)} %broadcast_in_dim.17), calls=%async_computation.2 | async-start | bytes 3145728 | tf_op jit(solution)/shard_map/all_to_all | solution.py:413
  89.3 2.7 %collective-permute-start.2 = (f32[4,384,256]{2,1,0:T(8,128)S(1)}, f32[4,384,256]{2,1,0:T(8,128)}, u32[]{:S(2)}, u32[]{:S(2)}) collective-permute-start(f32[4,384,256]{2,1,0:T(8,128)S(1)} %all-to-all-done.1.mine_ref), channel_id=1, source_target_pairs={{0,4},{4,0},{8,12},{12,8},{16,20},{20,16},{24,28},{28,24},{1,5},{5... | collective-permute-start | bytes 4718600 | tf_op jit(solution)/shard_map/ppermute | solution.py:412
  92.0 21.2 %shard_map.78 = (f32[512,512]{1,0:T(8,128)}, f32[2,256,256]{2,1,0:T(8,128)}, f32[128,256]{1,0:T(8,128)}) custom-call(s32[5]{0:T(128)} %stack.19.idx_ref, f32[512,512]{1,0:T(8,128)} %get-tuple-element.19.rest_ref, f32[128,256]{1,0:T(8,128)} %get-tuple-element.20.before_ref), custom_call_target="tpu_custom_call" | custom-call | flops 30000001024 | bytes 8388608 | tf_op jit(solution)/shard_map/pallas_call | solution.py:415
  113.2 0.0 all-to-all-done.2.own_ref
  113.3 0.0 collective-permute-done.2.other_ref
  113.3 0.0 copy-start.5
  113.3 16.7 %shard_map.79 = (f32[384,256]{1,0:T(8,128)}, f32[384,768]{1,0:T(8,128)}, f32[288,768]{1,0:T(8,128)}) custom-call(s32[5]{0:T(128)} %stack.19.idx_ref, f32[4,384,256]{2,1,0:T(8,128)} %all-to-all-done.2.own_ref, f32[4,384,256]{2,1,0:T(8,128)} %copy-done.3, f32[4,384,256]{2,1,0:T(8,128)} %collective-permute-done.2.other_ref, ...), custom_call_target="tpu_custom_call" | custom-call | flops 10000000000 | bytes 8388608 | tf_op jit(solution)/shard_map/pallas_call | solution.py:430
  130.0 4.6 %collective-permute-start.3 = (f32[288,768]{1,0:T(8,128)}, f32[288,768]{1,0:T(8,128)S(1)}, u32[]{:S(2)}, u32[]{:S(2)}) collective-permute-start(f32[288,768]{1,0:T(8,128)} %get-tuple-element.31), channel_id=1, source_target_pairs={{0,32},{32,0},{64,96},{96,64},{128,160},{160,128},{192,224},{224,1... | collective-permute-start | bytes 2654216 | tf_op jit(solution)/shard_map/ppermute | solution.py:454
  134.6 0.9 dynamic-slice_reduce_fusion
  135.6 0.1 copy.8.diag_ref
  135.7 0.0 copy-done
  135.8 0.0 copy-start.2
  135.8 1.3 copy-done.2
  137.0 2.9 %shard_map.80.base_ref = f32[288,1152]{1,0:T(8,128)S(1)} custom-call(s32[5]{0:T(128)S(1)} %copy-done, f32[384,768]{1,0:T(8,128)S(1)} %copy-done.2, s32[1,384]{1,0:T(1,128)S(1)} %copy-done.1, s32[2,384]{1,0:T(2,128)S(1)} %reshape.16.map_ref, f32[288,1]{1,0:T(8,128)S(1)} %copy.8.diag_ref), custom_call_target="tpu_custom_call" | custom-call | flops 2000000000 | bytes 8388608 | tf_op jit(solution)/shard_map/pallas_call | solution.py:460
  139.9 14.9 %collective-permute-done.3.got_ref = f32[288,768]{1,0:T(8,128)S(1)} collective-permute-done((f32[288,768]{1,0:T(8,128)}, f32[288,768]{1,0:T(8,128)S(1)}, u32[]{:S(2)}, u32[]{:S(2)}) %collective-permute-start.3) | collective-permute-done | bytes 884768 | tf_op jit(solution)/shard_map/ppermute | solution.py:454
  154.8 3.2 %shard_map.81 = f32[288,1152]{1,0:T(8,128)} custom-call(s32[5]{0:T(128)S(1)} %copy-done, f32[288,768]{1,0:T(8,128)S(1)} %collective-permute-done.3.got_ref, s32[2,384]{1,0:T(2,128)S(1)} %reshape.15.map_ref, f32[288,1152]{1,0:T(8,128)S(1)} %shard_map.80.base_ref), custom_call_target="tpu_custom_call" | custom-call | flops 2000000000 | bytes 8388608 | tf_op jit(solution)/shard_map/pallas_call | solution.py:467
  (8 shorter events, 0.0 us)
Async XLA Ops:
  3.7 6.9 %copy-start.4 = (f32[1,384,256]{2,1,0:T(8,128)S(1)}, f32[1,384,256]{2,1,0:T(8,128)}, u32[]{:S(2)}) copy-start(f32[1,384,256]{2,1,0:T(8,128)} %param.6) | copy-start | bytes 1179652
  3.7 42.7 %all-to-all-start = ((f32[16,160,128]{2,1,0:T(8,128)}), f32[16,160,128]{2,1,0:T(8,128)}, u32[]{:S(2)}, u32[]{:S(2)}) async-start(f32[16,160,128]{2,1,0:T(8,128)} %shard_map.76), calls=%async_computation | async-start | bytes 2621440 | tf_op jit(solution)/shard_map/all_to_all | solution.py:375
  10.6 35.7 %collective-permute-start = (f32[384,256]{1,0:T(8,128)S(1)}, f32[384,256]{1,0:T(8,128)S(1)}, u32[]{:S(2)}, u32[]{:S(2)}) collective-permute-start(f32[384,256]{1,0:T(8,128)S(1)} %bitcast.11), channel_id=1, source_target_pairs={{0,0},{1,8},{2,16},{3,24},{4,4},{5,12},{6,20},{7,28},{8,1},{9,9},{... | collective-permute-start | bytes 1179656 | tf_op jit(solution)/shard_map/ppermute | solution.py:379
  46.3 11.0 %collective-permute-start.1 = (f32[16,160,128]{2,1,0:T(8,128)}, f32[16,160,128]{2,1,0:T(8,128)}, u32[]{:S(2)}, u32[]{:S(2)}) collective-permute-start(f32[16,160,128]{2,1,0:T(8,128)} %all-to-all-done.mine_ref), channel_id=1, source_target_pairs={{0,4},{4,0},{8,12},{12,8},{16,20},{20,16},{24,28},{28,24},{1,5},{5... | collective-permute-start | bytes 3932168 | tf_op jit(solution)/shard_map/ppermute | solution.py:381
  52.1 31.5 %all-to-all-start.1 = ((f32[4,384,256]{2,1,0:T(8,128)}), f32[4,384,256]{2,1,0:T(8,128)S(1)}, u32[]{:S(2)}, u32[]{:S(2)}) async-start(f32[4,384,256]{2,1,0:T(8,128)} %broadcast_in_dim.16), calls=%async_computation.1 | async-start | bytes 3145728 | tf_op jit(solution)/shard_map/all_to_all | solution.py:383
  83.5 5.8 %copy-start.3 = (f32[4,384,256]{2,1,0:T(8,128)}, f32[4,384,256]{2,1,0:T(8,128)S(1)}, u32[]{:S(2)}) copy-start(f32[4,384,256]{2,1,0:T(8,128)S(1)} %all-to-all-done.1.mine_ref) | copy-start | bytes 4718596
  85.0 28.3 %all-to-all-start.2 = ((f32[4,384,256]{2,1,0:T(8,128)}), f32[4,384,256]{2,1,0:T(8,128)}, u32[]{:S(2)}, u32[]{:S(2)}) async-start(f32[4,384,256]{2,1,0:T(8,128)} %broadcast_in_dim.17), calls=%async_computation.2 | async-start | bytes 3145728 | tf_op jit(solution)/shard_map/all_to_all | solution.py:413
  89.3 23.9 %collective-permute-start.2 = (f32[4,384,256]{2,1,0:T(8,128)S(1)}, f32[4,384,256]{2,1,0:T(8,128)}, u32[]{:S(2)}, u32[]{:S(2)}) collective-permute-start(f32[4,384,256]{2,1,0:T(8,128)S(1)} %all-to-all-done.1.mine_ref), channel_id=1, source_target_pairs={{0,4},{4,0},{8,12},{12,8},{16,20},{20,16},{24,28},{28,24},{1,5},{5... | collective-permute-start | bytes 4718600 | tf_op jit(solution)/shard_map/ppermute | solution.py:412
  113.3 22.3 %copy-start.5 = (f32[1,288]{1,0:T(1,128)S(1)}, f32[1,288]{1,0:T(1,128)}, u32[]{:S(2)}) copy-start(f32[1,288]{1,0:T(1,128)} %param.9) | copy-start | bytes 3460
  113.3 22.5 %copy-start = (s32[5]{0:T(128)S(1)}, s32[5]{0:T(128)}, u32[]{:S(2)}) copy-start(s32[5]{0:T(128)} %stack.19.idx_ref) | copy-start | bytes 64
  113.3 22.5 %copy-start.1 = (s32[1,384]{1,0:T(1,128)S(1)}, s32[1,384]{1,0:T(1,128)}, u32[]{:S(2)}) copy-start(s32[1,384]{1,0:T(1,128)} %dynamic_slice.9.map_ref.row_map_ref) | copy-start | bytes 4612
  130.0 24.8 %collective-permute-start.3 = (f32[288,768]{1,0:T(8,128)}, f32[288,768]{1,0:T(8,128)S(1)}, u32[]{:S(2)}, u32[]{:S(2)}) collective-permute-start(f32[288,768]{1,0:T(8,128)} %get-tuple-element.31), channel_id=1, source_target_pairs={{0,32},{32,0},{64,96},{96,64},{128,160},{160,128},{192,224},{224,1... | collective-permute-start | bytes 2654216 | tf_op jit(solution)/shard_map/ppermute | solution.py:454
  135.8 1.3 copy-start.2

commit v3 on v2

v3 whole, which is shorter than its diff:
```python
import functools

import jax
import jax.numpy as jnp
from jax import lax
from jax.experimental import pallas as pl
from jax.experimental.pallas import tpu as pltpu
from jax.sharding import PartitionSpec as P

HI = lax.Precision.HIGHEST
F32 = jnp.float32
BF16 = jnp.bfloat16
B = 128
SB = 32
H = 64
PAYLOAD = 144
VMEM = pl.BlockSpec(memory_space=pltpu.VMEM)
HBM = pl.BlockSpec(memory_space=pltpu.HBM)
SMEM = pl.BlockSpec(memory_space=pltpu.SMEM)


def dot_tn(a, b, precision=HI):
    return lax.dot_general(a, b, (((0,), (0,)), ((), ())), precision=precision, preferred_element_type=F32)


def dot_nn(a, b, precision=HI):
    return lax.dot_general(a, b, (((1,), (0,)), ((), ())), precision=precision, preferred_element_type=F32)


def dot_nt(a, b, precision=HI):
    return lax.dot_general(a, b, (((1,), (1,)), ((), ())), precision=precision, preferred_element_type=F32)


def params(flops, mib=60):
    return dict(
        compiler_params=pltpu.CompilerParams(vmem_limit_bytes=mib * 2**20),
        cost_estimate=pl.CostEstimate(flops=flops, bytes_accessed=2**23, transcendentals=0),
    )


def pack_kernel(idx_ref, p_ref, o_ref):
    row, col = idx_ref[0], idx_ref[1]
    copies = o_ref.shape[0]

    def put(lo, value):
        for q in range(copies):
            o_ref[q, lo : lo + value.shape[0], :] = value

    for half in range(2):
        block = p_ref[:, half * B : half * B + B]
        other = 2 * col + half

        @pl.when(row < other)
        def _():
            put(half * H, block[0:H, :])

        @pl.when(row > other)
        def _():
            put(half * H, block[:, H:B].T)

        @pl.when(row == other)
        def _():
            q = H // 2
            put(half * H, block[0:q, :])
            put(half * H + q, jnp.concatenate([block[H : H + q, H : H + q], block[q:H, q:B]], axis=1))
            side = jnp.concatenate([block[H : H + q, H + q : B], block[H + q : B, H + q : B]], axis=1)
            put(2 * H, jnp.concatenate([side[0 : q // 2], side[q // 2 : q]], axis=1))


def unpack(src, parity, u_ref, nrow, ncol):
    for x in range(nrow // 2):
        i = 2 * x + parity
        for y in range(ncol):
            c = x * ncol + y
            for half in range(2):
                o = 2 * y + half
                piece = src[c, half * H : half * H + H, :]
                if i < o:
                    u_ref[i * B : i * B + H, o * B : o * B + B] = piece
                elif i > o:
                    u_ref[o * B + H : o * B + B, i * B : i * B + B] = piece
                else:
                    q = H // 2
                    u_ref[i * B : i * B + q, i * B : i * B + B] = piece[0:q]
                    u_ref[i * B + q : i * B + H, i * B : i * B + B] = jnp.concatenate(
                        [piece[0:q, q:H].T, piece[q:H, q:B]], axis=1
                    )
                    side = src[c, 2 * H : 2 * H + q // 2, :]
                    side = jnp.concatenate([side[:, 0:H], side[:, H:B]], axis=0)
                    right = jnp.concatenate(
                        [
                            jnp.concatenate([piece[q:H, 0:q], side[:, 0:q]], axis=1),
                            jnp.concatenate([side[:, 0:q].T, side[:, q:H]], axis=1),
                        ],
                        axis=0,
                    )
                    cross = jnp.concatenate([piece[0:q, H:B], piece[q:H, H:B]], axis=0).T
                    u_ref[i * B + H : i * B + B, i * B : i * B + B] = jnp.concatenate([cross, right], axis=1)


def spread_row(value, r):
    return jnp.broadcast_to(value[r : r + 1, :], (8, B))


def chain(s_ref, s):
    nb, r0 = SB // 8, s * SB
    rowid = lax.broadcasted_iota(jnp.int32, (8, B), 0)
    blk = [s_ref[r0 + 8 * b : r0 + 8 * b + 8, 0:B] for b in range(nb)]
    c = [
        [
            jnp.broadcast_to(blk[b][:, r0 + i : r0 + i + 1], (8, B)) if b >= i // 8 else None
            for b in range(nb)
        ]
        for i in range(SB)
    ]
    x = [[s_ref[r0 + 8 * b : r0 + 8 * b + 8, B * h : B * h + B] for h in range(2)] for b in range(nb)]
    pivots = [None] * nb
    for j in range(SB):
        bj, rj = j // 8, j % 8
        p = spread_row(c[j][bj], rj)
        inv = 1.0 / p
        pivots[bj] = p if pivots[bj] is None else jnp.where(rowid == rj, p, pivots[bj])
        for i in range(j + 1, SB):
            m = spread_row(c[j][i // 8], i % 8) * inv
            for b in range(i // 8, nb):
                c[i][b] = c[i][b] - c[j][b] * m
        for h in range(2):
            xr = spread_row(x[bj][h], rj) * inv
            for b in range(bj, nb):
                cm = c[j][b] if b > bj else jnp.where(rowid > rj, c[j][b], 0.0)
                x[b][h] = x[b][h] - cm * xr
    out = []
    for b in range(nb):
        q = lax.rsqrt(pivots[b])
        out.append(jnp.concatenate([x[b][0] * q, x[b][1] * q], axis=1))
    return jnp.concatenate(out, axis=0)


def factor_block(s_ref):
    for q in range(B // SB):
        p = chain(s_ref, q)
        s_ref[SB * q : SB * q + SB, :] = p
        below = SB * (q + 1)
        if below < B:
            s_ref[below:, :] = s_ref[below:, :] - dot_tn(p[:, below:B], p)


def chol_steps(u_ref, w_ref, s_ref, steps):
    n = u_ref.shape[0]
    ri = lax.broadcasted_iota(jnp.int32, (B, B), 0)
    ci = lax.broadcasted_iota(jnp.int32, (B, B), 1)
    eye = (ri == ci).astype(F32)

    def body(k, _):
        r0 = pl.multiple_of(k * B, B)
        s_ref[:, 0:B] = u_ref[pl.ds(r0, B), pl.ds(r0, B)]
        s_ref[:, B : 2 * B] = eye
        factor_block(s_ref)
        w = s_ref[:, B : 2 * B]
        for kk in range(steps):

            @pl.when(k == kk)
            def _():
                lo = (kk + 1) * B
                u_ref[kk * B : lo, kk * B : lo] = jnp.where(ri <= ci, s_ref[:, 0:B], 0.0)
                place = slice(kk % 2 * B, kk % 2 * B + B)
                w_ref[kk // 2, place, place] = w
                if lo < n:
                    panel = dot_nn(w, u_ref[kk * B : lo, lo:])
                    u_ref[kk * B : lo, lo:] = panel
                    for t in range(lo, n, 2 * B):
                        m = min(2 * B, n - t)
                        u_ref[t : t + m, t:] = u_ref[t : t + m, t:] - dot_tn(
                            panel[:, t - lo : t - lo + m], panel[:, t - lo :]
                        )

        return 0

    lax.fori_loop(0, steps, body, 0)
    for pair in range(steps // 2):
        lo = 2 * pair * B
        cross = dot_tn(u_ref[lo : lo + B, lo + B : lo + 2 * B], w_ref[pair, 0:B, 0:B])
        w_ref[pair, B : 2 * B, 0:B] = -dot_nn(w_ref[pair, B : 2 * B, B : 2 * B], cross)
        w_ref[pair, 0:B, B : 2 * B] = jnp.zeros((B, B), F32)


def lower_block(u_ref, l_ref, row, first_col, col):
    rows, cols = l_ref.shape
    start = pl.multiple_of((col - first_col) * cols, B)
    part = u_ref[pl.ds(start, cols), pl.ds(pl.multiple_of(row * rows - first_col * cols, B), rows)].T
    rl = lax.broadcasted_iota(jnp.int32, (rows, cols), 0) + row * rows
    cl = lax.broadcasted_iota(jnp.int32, (rows, cols), 1) + col * cols
    l_ref[...] = jnp.where(rl >= cl, part, 0.0)


def copy_all(sources, targets, sems):
    copies = [pltpu.make_async_copy(s, t, sems.at[i]) for i, (s, t) in enumerate(zip(sources, targets))]
    for copy in copies:
        copy.start()
    return copies


def chol_first(idx_ref, mine_ref, other_ref, top_ref, rest_ref, w_ref, l_ref, u_ref, v_ref, s_ref, sems):
    row, col, core = idx_ref[0], idx_ref[1], idx_ref[2]
    nblk = u_ref.shape[0] // B
    ncol = mine_ref.shape[0] // (nblk // 2)
    for parity in range(2):

        @pl.when(core == parity)
        def _():
            unpack(mine_ref, parity, u_ref, nblk, ncol)
            unpack(other_ref, 1 - parity, u_ref, nblk, ncol)

    chol_end(u_ref, v_ref, s_ref, sems, top_ref, rest_ref, w_ref, l_ref, row, col, 0)


def chol_next(first_col, idx_ref, from_ref, before_ref, *refs):
    if len(refs) == 8:
        top_ref, rest_ref, w_ref, l_ref, u_ref, v_ref, s_ref, sems = refs
    else:
        w_ref, l_ref, u_ref, v_ref, s_ref, sems = refs
        top_ref = rest_ref = None
    copy_all((from_ref,), (u_ref,), sems)[0].wait()
    l_ref[...] = before_ref[...]
    chol_end(u_ref, v_ref, s_ref, sems, top_ref, rest_ref, w_ref, l_ref, idx_ref[0], idx_ref[1], first_col)


def chol_end(u_ref, v_ref, s_ref, sems, top_ref, rest_ref, w_ref, l_ref, row, col, first_col):
    count = w_ref.shape[0]
    done = count * 2 * B
    left = u_ref.shape[0] - done
    chol_steps(u_ref, v_ref, s_ref, count * 2)
    sources, targets = (v_ref,), (w_ref,)
    if left > 0:
        sources += (u_ref.at[pl.ds(done, left), pl.ds(done, left)], u_ref.at[pl.ds(0, done)])
        targets += (rest_ref, top_ref)
    copies = copy_all(sources, targets, sems)
    rows, cols = l_ref.shape
    if first_col == 0:
        l_ref[...] = jnp.zeros_like(l_ref)

    @pl.when((col >= first_col) & (col < first_col + count) & (row * rows >= first_col * cols))
    def _():
        lower_block(u_ref, l_ref, row, first_col, col)

    for copy in copies:
        copy.wait()


def split3(value):
    first = value.astype(BF16)
    rest = value - first.astype(F32)
    second = rest.astype(BF16)
    third = (rest - second.astype(F32)).astype(BF16)
    return first, second, third


def pick_rows(onehot, parts):
    return sum(dot_nn(onehot, part, None) for part in reversed(parts))


def pick_cols(parts, onehot):
    return sum(dot_nt(part, onehot, None) for part in reversed(parts))


def split2(value):
    first = value.astype(BF16)
    return first, (value - first.astype(F32)).astype(BF16)


def dot3(dot, a, b):
    return dot(a[0], b[1], None) + dot(a[1], b[0], None) + dot(a[0], b[0], None)


def solve_kernel(
    idx_ref, own_ref, mine_ref, other_ref, top0_ref, top1_ref,
    w0_ref, w1_ref, w2_ref, upd_ref, map_ref,
    fb_ref, schur_ref, send_ref,
    x_ref, u0_ref, u1_ref, v_ref, fh_ref, fl_ref, t_ref, o_ref, sem, sems,
):
    row, col, core, side, leaf = idx_ref[0], idx_ref[1], idx_ref[2], idx_ref[3], idx_ref[5]
    ncol, rows, width = mine_ref.shape

    def load(y):
        cols = pl.ds(y * width, width)
        found = [pltpu.make_async_copy(own_ref.at[y], x_ref.at[pl.ds(0, rows), cols], sem.at[y, 0])]
        for c, ref in ((core, mine_ref), (1 - core, other_ref)):
            target = pl.ds(pl.multiple_of((1 + c) * rows, B), rows)
            which = 1 if ref is mine_ref else 2
            found.append(pltpu.make_async_copy(ref.at[y], x_ref.at[target, cols], sem.at[y, which]))
        inverse = (w0_ref.at[0], w1_ref.at[0], w1_ref.at[1], w2_ref.at[0])[y]
        found.append(pltpu.make_async_copy(inverse, v_ref.at[y], sem.at[y, 3]))
        if y == 0:
            found.append(pltpu.make_async_copy(top0_ref, u0_ref, sem.at[y, 4]))
        if y == 1:
            found.append(pltpu.make_async_copy(top1_ref, u1_ref, sem.at[y, 4]))
        for copy in found:
            copy.start()
        return found

    waiting = [load(y) for y in range(ncol)]
    trailing = pltpu.make_async_copy(upd_ref, t_ref, sems.at[0])
    trailing.start()
    cut = u0_ref.shape[0]
    for k in range(ncol):
        for copy in waiting[k]:
            copy.wait()
        lo, hi = k * width, (k + 1) * width
        x = x_ref[:, lo:hi]
        if k > 0:
            top = min(lo, cut)
            x = x - dot3(dot_nn, (fh_ref[:, 0:top], fl_ref[:, 0:top]), split2(u0_ref[0:top, lo:hi]))
            if lo > cut:
                above = split2(u1_ref[0 : lo - cut, lo - cut : hi - cut])
                x = x - dot3(dot_nn, (fh_ref[:, cut:lo], fl_ref[:, cut:lo]), above)
        f = dot3(dot_nt, split2(x), split2(v_ref[k]))
        fh_ref[:, lo:hi], fl_ref[:, lo:hi] = split2(f)

        @pl.when(col == k)
        def _():
            fb_ref[...] = f[0:rows]

    trailing.wait()
    schur = t_ref[...] - dot3(
        dot_nt, (fh_ref[0:rows, :], fl_ref[0:rows, :]), (fh_ref[rows:, :], fl_ref[rows:, :])
    )
    t_ref[...] = schur
    out = pltpu.make_async_copy(t_ref, schur_ref, sems.at[1])
    out.start()
    half = o_ref.shape[0]
    place = lax.broadcasted_iota(jnp.int32, (half, rows), 0) + (row * 2 + 1 - side) * half
    row_map = map_ref[pl.ds(leaf, 1), pl.ds(pl.multiple_of(row * rows, B), rows)]
    onehot = (place == row_map).astype(F32).astype(BF16)
    o_ref[...] = pick_rows(onehot, split3(schur))
    sent = pltpu.make_async_copy(o_ref, send_ref, sems.at[2])
    sent.start()
    out.wait()
    sent.wait()


def widen(value, maps, first, base):
    blocks = len(maps)
    width = value.shape[1] // blocks
    total = first.shape[1]
    step = total // blocks
    for b in range(blocks):
        lo = b * step // B * B
        hi = -((-(b + 1) * step) // B) * B
        place = lax.broadcasted_iota(jnp.int32, (hi - lo, width), 0) + (lo + base)
        onehot = (place == maps[b]).astype(F32).astype(BF16)
        first[:, lo:hi] = first[:, lo:hi] + pick_cols(split3(value[:, b * width : (b + 1) * width]), onehot)


def col_maps(map_ref, leaf, col, rows, cols):
    return [
        map_ref[pl.ds(leaf, 1), pl.ds(pl.multiple_of(col * cols + b * rows, B), rows)] for b in range(cols // rows)
    ]


def own_kernel(idx_ref, schur_ref, map_ref, diag_ref, o_ref):
    row, col, side, leaf = idx_ref[0], idx_ref[1], idx_ref[3], idx_ref[5]
    half, total = o_ref.shape
    rows, cols = schur_ref.shape
    rid = lax.broadcasted_iota(jnp.int32, (half, total), 0) + (row * 2 + side) * half
    cid = lax.broadcasted_iota(jnp.int32, (half, total), 1) + col * total
    o_ref[...] = jnp.where(rid == cid, diag_ref[...], 0.0)
    place = lax.broadcasted_iota(jnp.int32, (half, rows), 0) + (row * 2 + side) * half
    row_map = map_ref[pl.ds(leaf, 1), pl.ds(pl.multiple_of(row * rows, B), rows)]
    onehot = (place == row_map).astype(F32).astype(BF16)
    maps = col_maps(map_ref, leaf, col, rows, cols)
    widen(pick_rows(onehot, split3(schur_ref[...])), maps, o_ref, col * total)


def add_kernel(rows, idx_ref, got_ref, map_ref, base_ref, o_ref):
    side, leaf, col = idx_ref[3], idx_ref[5], idx_ref[1]
    o_ref[...] = base_ref[...]
    maps = col_maps(map_ref, leaf + 1 - 2 * side, col, rows, got_ref.shape[1])
    widen(got_ref[...], maps, o_ref, col * o_ref.shape[1])


def on_device(pivot, border, update, child_map, parent_diag):
    nrow, ncol = lax.axis_size("row"), lax.axis_size("col")
    row, col, leaf = lax.axis_index("row"), lax.axis_index("col"), lax.axis_index("leaf")
    nx = nrow // 2
    core, side = row % 2, leaf % 2
    idx = jnp.stack([row, col, core, side, jnp.int32(ncol), leaf]).astype(jnp.int32)
    piece_rows, piece_cols = pivot.shape[1:]
    n = piece_rows * nrow
    rows, width = border.shape[1:]
    half = parent_diag.shape[1]
    total = 2 * half * nrow // ncol
    upd_cols = update.shape[2]

    chips = nx * ncol
    packed = pl.pallas_call(
        pack_kernel,
        out_shape=jax.ShapeDtypeStruct((chips, PAYLOAD, B), F32),
        in_specs=[SMEM, VMEM],
        out_specs=VMEM,
        **params(10**6),
    )(idx, pivot[0])
    groups = [[(2 * x + c) * ncol + y for x in range(nx) for y in range(ncol)] for c in range(2)]
    mine = lax.all_to_all(packed, ("row", "col"), 0, 0, axis_index_groups=groups, tiled=True)
    swap = [(r, r ^ 1) for r in range(nrow)]

    turn = [((2 * x + c) * ncol + y, (2 * y + c) * ncol + x) for x in range(nx) for c in range(2) for y in range(ncol)]
    bord, mine = lax.optimization_barrier((border[0], mine))
    turned = lax.ppermute(bord, ("row", "col"), turn)
    other = lax.ppermute(mine, "row", swap)

    def factor(kernel, order, count, operands, specs, work):
        left = order - 2 * B * count
        square = lambda m: jax.ShapeDtypeStruct((m, m), F32)
        shapes = [square(left)] if left else []
        if left:
            shapes = [jax.ShapeDtypeStruct((2 * B * count, order), F32)] + shapes
        shapes += [
            jax.ShapeDtypeStruct((count, 2 * B, 2 * B), F32),
            jax.ShapeDtypeStruct((piece_rows, piece_cols), F32),
        ]
        return pl.pallas_call(
            kernel,
            out_shape=tuple(shapes),
            in_specs=[SMEM] + specs,
            out_specs=tuple([HBM] * (len(shapes) - 1) + [VMEM]),
            scratch_shapes=[
                pltpu.VMEM((order, order), F32),
                pltpu.VMEM((count, 2 * B, 2 * B), F32),
                pltpu.VMEM((B, 2 * B), F32),
                pltpu.SemaphoreType.DMA((3,)),
            ],
            **params(work, 58),
        )(idx, *operands)

    top0, rest, inv0, block = factor(chol_first, n, 1, (mine, other), [VMEM, VMEM], 10**10)

    bord, turned, inv0 = lax.optimization_barrier((bord, turned, inv0))
    same = [[2 * x + c for x in range(nx)] for c in range(2)]
    col_mine = lax.all_to_all(
        jnp.broadcast_to(turned, (nx, rows, width)), "row", 0, 0, axis_index_groups=same, tiled=True
    )

    middle = n // (2 * B) - 2
    top1, rest, inv1, block = factor(
        functools.partial(chol_next, 1), n - 2 * B, middle, (rest, block), [HBM, VMEM], 2 * 10**10
    )
    col_mine, rest, bord = lax.optimization_barrier((col_mine, rest, bord))
    col_other = lax.ppermute(col_mine, "row", swap)
    own = lax.all_to_all(jnp.broadcast_to(bord, (ncol, rows, width)), "col", 0, 0, tiled=True)
    inv2, pivot_out = factor(functools.partial(chol_next, 1 + middle), 2 * B, 1, (rest, block), [HBM, VMEM], 10**10)

    border_out, schur, send = pl.pallas_call(
        solve_kernel,
        out_shape=(
            jax.ShapeDtypeStruct((rows, width), F32),
            jax.ShapeDtypeStruct((rows, upd_cols), F32),
            jax.ShapeDtypeStruct((half, upd_cols), F32),
        ),
        in_specs=[SMEM] + [HBM] * 9 + [VMEM],
        out_specs=(VMEM, HBM, HBM),
        scratch_shapes=[
            pltpu.VMEM((3 * rows, n), F32),
            pltpu.VMEM(top0.shape, F32),
            pltpu.VMEM(top1.shape, F32),
            pltpu.VMEM((ncol, 2 * B, 2 * B), F32),
            pltpu.VMEM((3 * rows, n), BF16),
            pltpu.VMEM((3 * rows, n), BF16),
            pltpu.VMEM((rows, upd_cols), F32),
            pltpu.VMEM((half, upd_cols), F32),
            pltpu.SemaphoreType.DMA((ncol, 5)),
            pltpu.SemaphoreType.DMA((3,)),
        ],
        **params(10**10),
    )(idx, own, col_mine, col_other, top0, top1, inv0, inv1, inv2, update[0], child_map)

    got = lax.ppermute(send, "leaf", [(s, s ^ 1) for s in range(lax.axis_size("leaf"))])
    base = pl.pallas_call(
        own_kernel,
        out_shape=jax.ShapeDtypeStruct((half, total), F32),
        in_specs=[SMEM] + [VMEM] * 3,
        out_specs=VMEM,
        **params(2 * 10**9, 16),
    )(idx, schur, child_map, parent_diag.reshape(half, 1))
    parent_out = pl.pallas_call(
        functools.partial(add_kernel, rows),
        out_shape=jax.ShapeDtypeStruct((half, total), F32),
        in_specs=[SMEM] + [VMEM] * 3,
        out_specs=VMEM,
        **params(2 * 10**9, 16),
    )(idx, got, child_map, base)
    return pivot_out[None], border_out[None], parent_out[None]


def solution(mesh):
    placed = (
        P("leaf", "row", "col"),
        P("leaf", "row", "col"),
        P("leaf", "row", "col"),
        P(),
        P("leaf", "row"),
    )
    return jax.shard_map(
        on_device,
        mesh=mesh,
        in_specs=placed,
        out_specs=(P("leaf", "row", "col"), P("leaf", "row", "col"), P("leaf", "row", "col")),
        check_vma=False,
    )
```

time: 159 us -> 158 us (level)
  blocking collectives: 0 us -> 20.6 us
  waiting for transfers between devices: 46.3 us -> 26.5 us
  starting transfers between devices: 31.2 us -> 24.4 us
  Pallas kernels: 72.6 us -> 76.9 us
    ppermute x1, waiting for transfers between devices: 31.4 us -> 2.26 us  [on_device(): turned = lax.ppermute(bord, ('row', 'col'), turn)]
    all_to_all x0 -> x1, blocking collectives: none -> 20.6 us  [on_device(): lax.all_to_all(packed, ('row', 'col'), 0, 0, axis_index_groups=groups, ti...]
    all_to_all x1, waiting for transfers between devices: 0.01 us -> 9.37 us  [on_device(): lax.all_to_all(jnp.broadcast_to(bord, (ncol, rows, width)), 'col', 0, 0,...]
    all_to_all x1 -> x0, starting transfers between devices: 6.94 us -> none  [on_device(): lax.all_to_all(packed, ('row', 'col'), 0, 0, axis_index_groups=groups, ti...]
    pallas_call x3 -> x4, Pallas kernels: 50.6 us -> 55.3 us  [the longest x3 52.1 us: factor(): pl.pallas_call(kernel, out_shape=tuple(shapes), in_specs=[SMEM] + specs,...]
    dynamic_slice x2 -> x0, local copies, waits for them, and re-layouts: 2.26 us -> none  [the longest x1 1.36 us: on_device(): maps = lax.dynamic_slice(child_map, (leaf, row * rows), (1, rows))]
    unnamed x12 -> x18, local copies, waits for them, and re-layouts: 1.29 us -> 3.54 us
  transfers between devices with their start and end apart: 7 -> 6, of which waited for: 2 -> 3; matrix products, arithmetic and copies ran while one was open for 2% -> 1% of each run, Pallas kernels for 32% -> 35%
where the time goes in v3:
time: 158 us; the launch traced here: 156 us
  Pallas kernels  76.9 us (49%)
  waiting for transfers between devices  26.5 us (17%)
  starting transfers between devices  24.4 us (15%)
  blocking collectives  20.6 us (13%)
  local copies, waits for them, and re-layouts  6.96 us (4%)
    pallas_call x3, Pallas kernels, factor(): pl.pallas_call(kernel, out_shape=tuple(shapes), in_specs=[SMEM] + specs,...  52.1 us
    all_to_all x1, blocking collectives, on_device(): lax.all_to_all(packed, ('row', 'col'), 0, 0, axis_index_groups=groups, ti...  20.6 us
    pallas_call x1, Pallas kernels, on_device(): pl.pallas_call(solve_kernel, out_shape=(jax.ShapeDtypeStruct((rows, width...  16.3 us
    ppermute x1, waiting for transfers between devices, on_device(): lax.ppermute(send, 'leaf', [(s, s ^ 1) for s in range(lax.axis_size('leaf...  14.9 us
    all_to_all x1, waiting for transfers between devices, on_device(): lax.all_to_all(jnp.broadcast_to(bord, (ncol, rows, width)), 'col', 0, 0,...  9.37 us
    ppermute x1, starting transfers between devices, on_device(): other = lax.ppermute(mine, 'row', swap)  5.77 us
    ppermute x1, starting transfers between devices, on_device(): turned = lax.ppermute(bord, ('row', 'col'), turn)  4.39 us
    all_to_all x1, starting transfers between devices, on_device(): lax.all_to_all(jnp.broadcast_to(turned, (nx, rows, width)), 'row', 0, 0,...  3.94 us
  transfers between devices with their start and end apart: 6, of which 3 were waited for; matrix products, arithmetic and copies ran while one was open for 1% of the time, Pallas kernels for 35%

profile of v3, /device:TPU:7, one launch (start us, length us, event | category | flops | bytes accessed | tf_op | source)
XLA Modules:
  0.0 156.1 jit_solution(9332677911353181187)
XLA Ops:
  0.6 0.6 stack.23.idx_ref
  1.3 2.3 %shard_map.76 = f32[16,144,128]{2,1,0:T(8,128)} custom-call(s32[6]{0:T(128)} %stack.23.idx_ref, f32[128,256]{1,0:T(8,128)} %bitcast.14), custom_call_target="tpu_custom_call" | custom-call | flops 1000000 | bytes 8388608 | tf_op jit(solution)/shard_map/pallas_call | solution.py:395
  3.6 20.6 %all_to_all.15.mine_ref = f32[16,144,128]{2,1,0:T(8,128)S(1)} all-to-all(f32[16,144,128]{2,1,0:T(8,128)} %shard_map.76), channel_id=1, replica_groups={{0,1,2,3,8,9,10,11,16,17,18,19,24,25,26,27},{4,5,6,7,12,13,14,15,20,21,..., dimensions={0} | all-to-all | bytes 2359296 | tf_op jit(solution)/shard_map/all_to_all | solution.py:403
  24.2 5.8 %collective-permute-start.1 = (f32[16,144,128]{2,1,0:T(8,128)S(1)}, f32[16,144,128]{2,1,0:T(8,128)S(1)}, u32[]{:S(2)}, u32[]{:S(2)}) collective-permute-start(f32[16,144,128]{2,1,0:T(8,128)S(1)} %all_to_all.15.mine_ref), channel_id=1, source_target_pairs={{0,4},{4,0},{8,12},{12,8},{16,20},{20,16},{24,28},{28,24},{1,5},{5... | collective-permute-start | bytes 3538952 | tf_op jit(solution)/shard_map/ppermute | solution.py:409
  30.0 0.0 copy-done.6
  30.0 4.4 %collective-permute-start = (f32[384,256]{1,0:T(8,128)S(1)}, f32[384,256]{1,0:T(8,128)S(1)}, u32[]{:S(2)}, u32[]{:S(2)}) collective-permute-start(f32[384,256]{1,0:T(8,128)S(1)} %bitcast.12), channel_id=1, source_target_pairs={{0,0},{1,8},{2,16},{3,24},{4,4},{5,12},{6,20},{7,28},{8,1},{9,9},{... | collective-permute-start | bytes 1179656 | tf_op jit(solution)/shard_map/ppermute | solution.py:408
  34.4 0.0 collective-permute-done.1.other_ref
  34.4 0.0 copy-done.5
  34.4 0.0 copy-start.8
  34.4 1.0 copy-done.8
  35.4 16.8 %shard_map.77 = (f32[256,1024]{1,0:T(8,128)}, f32[768,768]{1,0:T(8,128)}, f32[1,256,256]{2,1,0:T(8,128)}, f32[128,256]{1,0:T(8,128)}) custom-call(s32[6]{0:T(128)} %stack.23.idx_ref, f32[16,144,128]{2,1,0:T(8,128)} %copy-done.5, f32[16,144,128]{2,1,0:T(8,128)} %copy-done.8), custom_call_target="tpu_custom_call" | custom-call | flops 10000000000 | bytes 8388608 | tf_op jit(solution)/shard_map/pallas_call | solution.py:421
  52.2 2.3 %collective-permute-done = f32[384,256]{1,0:T(8,128)S(1)} collective-permute-done((f32[384,256]{1,0:T(8,128)S(1)}, f32[384,256]{1,0:T(8,128)S(1)}, u32[]{:S(2)}, u32[]{:S(2)}) %collective-permute-start) | collective-permute-done | bytes 393248 | tf_op jit(solution)/shard_map/ppermute | solution.py:408
  54.4 1.3 broadcast_in_dim.15
  55.7 3.9 %all-to-all-start.1 = ((f32[4,384,256]{2,1,0:T(8,128)}), f32[4,384,256]{2,1,0:T(8,128)S(1)}, u32[]{:S(2)}, u32[]{:S(2)}) async-start(f32[4,384,256]{2,1,0:T(8,128)} %broadcast_in_dim.15), calls=%async_computation.1 | async-start | bytes 3145728 | tf_op jit(solution)/shard_map/all_to_all | solution.py:439
  59.7 23.9 %shard_map.78 = (f32[512,768]{1,0:T(8,128)}, f32[256,256]{1,0:T(8,128)}, f32[2,256,256]{2,1,0:T(8,128)}, f32[128,256]{1,0:T(8,128)}) custom-call(s32[6]{0:T(128)} %stack.23.idx_ref, f32[768,768]{1,0:T(8,128)} %get-tuple-element.28.from_ref, f32[128,256]{1,0:T(8,128)} %get-tuple-element.29.before_ref), custom_call_target="tpu_custom_call" | custom-call | flops 20000000000 | bytes 8388608 | tf_op jit(solution)/shard_map/pallas_call | solution.py:421
  83.6 0.0 all-to-all-done.1.mine_ref
  83.6 0.0 copy-start.3
  83.6 3.2 %collective-permute-start.2 = (f32[4,384,256]{2,1,0:T(8,128)S(1)}, f32[4,384,256]{2,1,0:T(8,128)}, u32[]{:S(2)}, u32[]{:S(2)}) collective-permute-start(f32[4,384,256]{2,1,0:T(8,128)S(1)} %all-to-all-done.1.mine_ref), channel_id=1, source_target_pairs={{0,4},{4,0},{8,12},{12,8},{16,20},{20,16},{24,28},{28,24},{1,5},{5... | collective-permute-start | bytes 4718600 | tf_op jit(solution)/shard_map/ppermute | solution.py:448
  86.8 1.4 broadcast_in_dim.17
  88.2 3.6 %all-to-all-start.2 = ((f32[4,384,256]{2,1,0:T(8,128)}), f32[4,384,256]{2,1,0:T(8,128)S(1)}, u32[]{:S(2)}, u32[]{:S(2)}) async-start(f32[4,384,256]{2,1,0:T(8,128)} %broadcast_in_dim.17), calls=%async_computation.2 | async-start | bytes 3145728 | tf_op jit(solution)/shard_map/all_to_all | solution.py:449
  91.7 11.4 %shard_map.79 = (f32[1,256,256]{2,1,0:T(8,128)}, f32[128,256]{1,0:T(8,128)}) custom-call(s32[6]{0:T(128)} %stack.23.idx_ref, f32[256,256]{1,0:T(8,128)} %get-tuple-element.32.from_ref, f32[128,256]{1,0:T(8,128)} %get-tuple-element.33.before_ref), custom_call_target="tpu_custom_call" | custom-call | flops 10000000000 | bytes 8388608 | tf_op jit(solution)/shard_map/pallas_call | solution.py:421
  103.2 9.4 %all-to-all-done.2.own_ref = f32[4,384,256]{2,1,0:T(8,128)S(1)} async-done(((f32[4,384,256]{2,1,0:T(8,128)}), f32[4,384,256]{2,1,0:T(8,128)S(1)}, u32[]{:S(2)}, u32[]{:S(2)}) %all-to-all-start.2) | async-done | bytes 1572896 | tf_op jit(solution)/shard_map/all_to_all | solution.py:449
  112.5 0.0 collective-permute-done.2.other_ref
  112.5 1.2 copy-done.4
  113.8 16.3 %shard_map.80 = (f32[384,256]{1,0:T(8,128)}, f32[384,768]{1,0:T(8,128)}, f32[288,768]{1,0:T(8,128)}) custom-call(s32[6]{0:T(128)} %stack.23.idx_ref, f32[4,384,256]{2,1,0:T(8,128)} %copy-done.4, f32[4,384,256]{2,1,0:T(8,128)} %copy-done.3, f32[4,384,256]{2,1,0:T(8,128)} %collective-permute-done.2.other_ref, f32[256,1024]{1,0:T(8,128)} %get-tuple-element.37.top0_ref, ...), custom_call_target="tpu_custom_call" | custom-call | flops 10000000000 | bytes 8388608 | tf_op jit(solution)/shard_map/pallas_call | solution.py:452
  130.1 3.5 %collective-permute-start.3 = (f32[288,768]{1,0:T(8,128)}, f32[288,768]{1,0:T(8,128)S(1)}, u32[]{:S(2)}, u32[]{:S(2)}) collective-permute-start(f32[288,768]{1,0:T(8,128)} %get-tuple-element.43), channel_id=1, source_target_pairs={{0,32},{32,0},{64,96},{96,64},{128,160},{160,128},{192,224},{224,1... | collective-permute-start | bytes 2654216 | tf_op jit(solution)/shard_map/ppermute | solution.py:476
  133.7 0.1 copy.8.diag_ref
  133.8 0.0 copy-start.2
  133.8 1.3 copy-done.2
  135.1 2.9 %shard_map.81.base_ref = f32[288,1152]{1,0:T(8,128)S(1)} custom-call(s32[6]{0:T(128)S(1)} %copy-done, f32[384,768]{1,0:T(8,128)S(1)} %copy-done.2, s32[16,3072]{1,0:T(8,128)S(1)} %copy-done.1, f32[288,1]{1,0:T(8,128)S(1)} %copy.8.diag_ref), custom_call_target="tpu_custom_call" | custom-call | flops 2000000000 | bytes 8388608 | tf_op jit(solution)/shard_map/pallas_call | solution.py:477
  138.0 14.9 %collective-permute-done.3.got_ref = f32[288,768]{1,0:T(8,128)S(1)} collective-permute-done((f32[288,768]{1,0:T(8,128)}, f32[288,768]{1,0:T(8,128)S(1)}, u32[]{:S(2)}, u32[]{:S(2)}) %collective-permute-start.3) | collective-permute-done | bytes 884768 | tf_op jit(solution)/shard_map/ppermute | solution.py:476
  152.9 3.2 %shard_map.82 = f32[288,1152]{1,0:T(8,128)} custom-call(s32[6]{0:T(128)S(1)} %copy-done, f32[288,768]{1,0:T(8,128)S(1)} %collective-permute-done.3.got_ref, s32[16,3072]{1,0:T(8,128)S(1)} %copy-done.1, f32[288,1152]{1,0:T(8,128)S(1)} %shard_map.81.base_ref), custom_call_target="tpu_custom_call" | custom-call | flops 2000000000 | bytes 8388608 | tf_op jit(solution)/shard_map/pallas_call | solution.py:484
  (10 shorter events, 0.0 us)
Async XLA Ops:
  1.3 28.7 %copy-start.6 = (f32[1,384,256]{2,1,0:T(8,128)S(1)}, f32[1,384,256]{2,1,0:T(8,128)}, u32[]{:S(2)}) copy-start(f32[1,384,256]{2,1,0:T(8,128)} %param.6) | copy-start | bytes 1179652
  24.2 10.2 %copy-start.5 = (f32[16,144,128]{2,1,0:T(8,128)}, f32[16,144,128]{2,1,0:T(8,128)S(1)}, u32[]{:S(2)}) copy-start(f32[16,144,128]{2,1,0:T(8,128)S(1)} %all_to_all.15.mine_ref) | copy-start | bytes 3538948
  24.2 10.2 %collective-permute-start.1 = (f32[16,144,128]{2,1,0:T(8,128)S(1)}, f32[16,144,128]{2,1,0:T(8,128)S(1)}, u32[]{:S(2)}, u32[]{:S(2)}) collective-permute-start(f32[16,144,128]{2,1,0:T(8,128)S(1)} %all_to_all.15.mine_ref), channel_id=1, source_target_pairs={{0,4},{4,0},{8,12},{12,8},{16,20},{20,16},{24,28},{28,24},{1,5},{5... | collective-permute-start | bytes 3538952 | tf_op jit(solution)/shard_map/ppermute | solution.py:409
  30.0 24.5 %collective-permute-start = (f32[384,256]{1,0:T(8,128)S(1)}, f32[384,256]{1,0:T(8,128)S(1)}, u32[]{:S(2)}, u32[]{:S(2)}) collective-permute-start(f32[384,256]{1,0:T(8,128)S(1)} %bitcast.12), channel_id=1, source_target_pairs={{0,0},{1,8},{2,16},{3,24},{4,4},{5,12},{6,20},{7,28},{8,1},{9,9},{... | collective-permute-start | bytes 1179656 | tf_op jit(solution)/shard_map/ppermute | solution.py:408
  34.4 1.0 copy-start.8
  55.7 27.9 %all-to-all-start.1 = ((f32[4,384,256]{2,1,0:T(8,128)}), f32[4,384,256]{2,1,0:T(8,128)S(1)}, u32[]{:S(2)}, u32[]{:S(2)}) async-start(f32[4,384,256]{2,1,0:T(8,128)} %broadcast_in_dim.15), calls=%async_computation.1 | async-start | bytes 3145728 | tf_op jit(solution)/shard_map/all_to_all | solution.py:439
  83.6 4.6 %copy-start.3 = (f32[4,384,256]{2,1,0:T(8,128)}, f32[4,384,256]{2,1,0:T(8,128)S(1)}, u32[]{:S(2)}) copy-start(f32[4,384,256]{2,1,0:T(8,128)S(1)} %all-to-all-done.1.mine_ref) | copy-start | bytes 4718596
  83.6 28.9 %collective-permute-start.2 = (f32[4,384,256]{2,1,0:T(8,128)S(1)}, f32[4,384,256]{2,1,0:T(8,128)}, u32[]{:S(2)}, u32[]{:S(2)}) collective-permute-start(f32[4,384,256]{2,1,0:T(8,128)S(1)} %all-to-all-done.1.mine_ref), channel_id=1, source_target_pairs={{0,4},{4,0},{8,12},{12,8},{16,20},{20,16},{24,28},{28,24},{1,5},{5... | collective-permute-start | bytes 4718600 | tf_op jit(solution)/shard_map/ppermute | solution.py:448
  88.2 24.4 %all-to-all-start.2 = ((f32[4,384,256]{2,1,0:T(8,128)}), f32[4,384,256]{2,1,0:T(8,128)S(1)}, u32[]{:S(2)}, u32[]{:S(2)}) async-start(f32[4,384,256]{2,1,0:T(8,128)} %broadcast_in_dim.17), calls=%async_computation.2 | async-start | bytes 3145728 | tf_op jit(solution)/shard_map/all_to_all | solution.py:449
  112.5 1.2 copy-start.4
  113.8 19.9 %copy-start.7 = (f32[1,288]{1,0:T(1,128)S(1)}, f32[1,288]{1,0:T(1,128)}, u32[]{:S(2)}) copy-start(f32[1,288]{1,0:T(1,128)} %param.9) | copy-start | bytes 3460
  113.8 20.0 %copy-start = (s32[6]{0:T(128)S(1)}, s32[6]{0:T(128)}, u32[]{:S(2)}) copy-start(s32[6]{0:T(128)} %stack.23.idx_ref) | copy-start | bytes 76
  113.8 20.1 %copy-start.1 = (s32[16,3072]{1,0:T(8,128)S(1)}, s32[16,3072]{1,0:T(8,128)}, u32[]{:S(2)}) copy-start(s32[16,3072]{1,0:T(8,128)} %map_ref.5) | copy-start | bytes 589828
  130.1 22.7 %collective-permute-start.3 = (f32[288,768]{1,0:T(8,128)}, f32[288,768]{1,0:T(8,128)S(1)}, u32[]{:S(2)}, u32[]{:S(2)}) collective-permute-start(f32[288,768]{1,0:T(8,128)} %get-tuple-element.43), channel_id=1, source_target_pairs={{0,32},{32,0},{64,96},{96,64},{128,160},{160,128},{192,224},{224,1... | collective-permute-start | bytes 2654216 | tf_op jit(solution)/shard_map/ppermute | solution.py:476
  133.8 1.3 copy-start.2

commit v4 on v3

--- a/solution.py
+++ b/solution.py
@@ -215,14 +215,10 @@
 
 
 def chol_next(first_col, idx_ref, from_ref, before_ref, *refs):
-    if len(refs) == 8:
-        top_ref, rest_ref, w_ref, l_ref, u_ref, v_ref, s_ref, sems = refs
-    else:
-        w_ref, l_ref, u_ref, v_ref, s_ref, sems = refs
-        top_ref = rest_ref = None
+    top_ref, w_ref, l_ref, u_ref, v_ref, s_ref, sems = refs
     copy_all((from_ref,), (u_ref,), sems)[0].wait()
     l_ref[...] = before_ref[...]
-    chol_end(u_ref, v_ref, s_ref, sems, top_ref, rest_ref, w_ref, l_ref, idx_ref[0], idx_ref[1], first_col)
+    chol_end(u_ref, v_ref, s_ref, sems, top_ref, None, w_ref, l_ref, idx_ref[0], idx_ref[1], first_col)
 
 
 def chol_end(u_ref, v_ref, s_ref, sems, top_ref, rest_ref, w_ref, l_ref, row, col, first_col):
@@ -230,10 +226,10 @@
     done = count * 2 * B
     left = u_ref.shape[0] - done
     chol_steps(u_ref, v_ref, s_ref, count * 2)
-    sources, targets = (v_ref,), (w_ref,)
+    sources, targets = (v_ref, u_ref.at[pl.ds(0, done)]), (w_ref, top_ref)
     if left > 0:
-        sources += (u_ref.at[pl.ds(done, left), pl.ds(done, left)], u_ref.at[pl.ds(0, done)])
-        targets += (rest_ref, top_ref)
+        sources += (u_ref.at[pl.ds(done, left), pl.ds(done, left)],)
+        targets += (rest_ref,)
     copies = copy_all(sources, targets, sems)
     rows, cols = l_ref.shape
     if first_col == 0:
@@ -272,39 +268,11 @@
     return dot(a[0], b[1], None) + dot(a[1], b[0], None) + dot(a[0], b[0], None)
 
 
-def solve_kernel(
-    idx_ref, own_ref, mine_ref, other_ref, top0_ref, top1_ref,
-    w0_ref, w1_ref, w2_ref, upd_ref, map_ref,
-    fb_ref, schur_ref, send_ref,
-    x_ref, u0_ref, u1_ref, v_ref, fh_ref, fl_ref, t_ref, o_ref, sem, sems,
-):
-    row, col, core, side, leaf = idx_ref[0], idx_ref[1], idx_ref[2], idx_ref[3], idx_ref[5]
-    ncol, rows, width = mine_ref.shape
-
-    def load(y):
-        cols = pl.ds(y * width, width)
-        found = [pltpu.make_async_copy(own_ref.at[y], x_ref.at[pl.ds(0, rows), cols], sem.at[y, 0])]
-        for c, ref in ((core, mine_ref), (1 - core, other_ref)):
-            target = pl.ds(pl.multiple_of((1 + c) * rows, B), rows)
-            which = 1 if ref is mine_ref else 2
-            found.append(pltpu.make_async_copy(ref.at[y], x_ref.at[target, cols], sem.at[y, which]))
-        inverse = (w0_ref.at[0], w1_ref.at[0], w1_ref.at[1], w2_ref.at[0])[y]
-        found.append(pltpu.make_async_copy(inverse, v_ref.at[y], sem.at[y, 3]))
-        if y == 0:
-            found.append(pltpu.make_async_copy(top0_ref, u0_ref, sem.at[y, 4]))
-        if y == 1:
-            found.append(pltpu.make_async_copy(top1_ref, u1_ref, sem.at[y, 4]))
-        for copy in found:
-            copy.start()
-        return found
-
-    waiting = [load(y) for y in range(ncol)]
-    trailing = pltpu.make_async_copy(upd_ref, t_ref, sems.at[0])
-    trailing.start()
+def solve_rows(x_ref, fh_ref, fl_ref, u0_ref, u1_ref, v_ref, ready, done):
     cut = u0_ref.shape[0]
-    for k in range(ncol):
-        for copy in waiting[k]:
-            copy.wait()
+    count, width = v_ref.shape[:2]
+    for k in range(count):
+        ready(k)
         lo, hi = k * width, (k + 1) * width
         x = x_ref[:, lo:hi]
         if k > 0:
@@ -315,30 +283,118 @@
                 x = x - dot3(dot_nn, (fh_ref[:, cut:lo], fl_ref[:, cut:lo]), above)
         f = dot3(dot_nt, split2(x), split2(v_ref[k]))
         fh_ref[:, lo:hi], fl_ref[:, lo:hi] = split2(f)
-
+        done(k, f)
+
+
+def load_factor(y, top0_ref, top1_ref, w0_ref, w1_ref, u0_ref, u1_ref, v_ref, sem):
+    early = w0_ref.shape[0]
+    inverse = w0_ref.at[y] if y < early else w1_ref.at[y - early]
+    found = [pltpu.make_async_copy(inverse, v_ref.at[y], sem.at[y, 0])]
+    if y == 0:
+        found.append(pltpu.make_async_copy(top0_ref, u0_ref, sem.at[y, 1]))
+    if y == 1:
+        found.append(pltpu.make_async_copy(top1_ref, u1_ref, sem.at[y, 1]))
+    return found
+
+
+def solve_first(
+    idx_ref, own0_ref, own1_ref, own2_ref, own3_ref, mine_ref, top0_ref, top1_ref, w0_ref, w1_ref, upd_ref,
+    fb_ref, oh_ref, ol_ref, part_ref,
+    x_ref, u0_ref, u1_ref, v_ref, fh_ref, fl_ref, t_ref, sem, sems,
+):
+    col, core = idx_ref[1], idx_ref[2]
+    ncol, rows, width = mine_ref.shape
+    waiting = []
+    for y in range(ncol):
+        found = load_factor(y, top0_ref, top1_ref, w0_ref, w1_ref, u0_ref, u1_ref, v_ref, sem)
+        cols = pl.ds(y * width, width)
+        found.append(pltpu.make_async_copy(mine_ref.at[y], x_ref.at[pl.ds(rows, rows), cols], sem.at[y, 2]))
+        if y == 0:
+            for d, ref in enumerate((own0_ref, own1_ref, own2_ref, own3_ref)):
+                whose = lax.rem(col + ncol - d, ncol)
+                target = pl.ds(pl.multiple_of(whose * width, B), width)
+                found.append(pltpu.make_async_copy(ref, x_ref.at[pl.ds(0, rows), target], sem.at[d, 3]))
+        for copy in found:
+            copy.start()
+        waiting.append(found)
+    columns = pl.ds(pl.multiple_of(core * rows, B), rows)
+    trailing = pltpu.make_async_copy(upd_ref.at[:, columns], t_ref, sems.at[0])
+    trailing.start()
+
+    def ready(k):
+        for copy in waiting[k]:
+            copy.wait()
+
+    def done(k, f):
         @pl.when(col == k)
         def _():
             fb_ref[...] = f[0:rows]
 
+    solve_rows(x_ref, fh_ref, fl_ref, u0_ref, u1_ref, v_ref, ready, done)
+    out = [
+        pltpu.make_async_copy(fh_ref.at[pl.ds(0, rows)], oh_ref, sems.at[1]),
+        pltpu.make_async_copy(fl_ref.at[pl.ds(0, rows)], ol_ref, sems.at[2]),
+    ]
+    for copy in out:
+        copy.start()
     trailing.wait()
-    schur = t_ref[...] - dot3(
+    t_ref[...] = t_ref[...] - dot3(
         dot_nt, (fh_ref[0:rows, :], fl_ref[0:rows, :]), (fh_ref[rows:, :], fl_ref[rows:, :])
     )
-    t_ref[...] = schur
-    out = pltpu.make_async_copy(t_ref, schur_ref, sems.at[1])
+    out.append(pltpu.make_async_copy(t_ref, part_ref, sems.at[3]))
+    out[-1].start()
+    for copy in out:
+        copy.wait()
+
+
+def solve_last(
+    idx_ref, other_ref, oh_ref, ol_ref, part_ref, top0_ref, top1_ref, w0_ref, w1_ref, upd_ref, map_ref,
+    schur_ref, send_ref,
+    x_ref, u0_ref, u1_ref, v_ref, fh_ref, fl_ref, rh_ref, rl_ref, t_ref, o_ref, sem, sems,
+):
+    row, core, side, leaf = idx_ref[0], idx_ref[2], idx_ref[3], idx_ref[5]
+    ncol, rows, width = other_ref.shape
+    waiting = []
+    for y in range(ncol):
+        found = load_factor(y, top0_ref, top1_ref, w0_ref, w1_ref, u0_ref, u1_ref, v_ref, sem)
+        found.append(pltpu.make_async_copy(other_ref.at[y], x_ref.at[:, pl.ds(y * width, width)], sem.at[y, 2]))
+        for copy in found:
+            copy.start()
+        waiting.append(found)
+    mine = pl.ds(pl.multiple_of(core * rows, B), rows)
+    rest = pl.ds(pl.multiple_of((1 - core) * rows, B), rows)
+    later = [
+        pltpu.make_async_copy(oh_ref, rh_ref, sems.at[0]),
+        pltpu.make_async_copy(ol_ref, rl_ref, sems.at[1]),
+        pltpu.make_async_copy(part_ref, t_ref.at[:, mine], sems.at[2]),
+        pltpu.make_async_copy(upd_ref.at[:, rest], t_ref.at[:, rest], sems.at[3]),
+    ]
+    for copy in later:
+        copy.start()
+
+    def ready(k):
+        for copy in waiting[k]:
+            copy.wait()
+
+    solve_rows(x_ref, fh_ref, fl_ref, u0_ref, u1_ref, v_ref, ready, lambda k, f: None)
+    for copy in later:
+        copy.wait()
+    product = dot3(dot_nt, (rh_ref[...], rl_ref[...]), (fh_ref[...], fl_ref[...]))
+    t_ref[:, rest] = t_ref[:, rest] - product
+    out = pltpu.make_async_copy(t_ref, schur_ref, sems.at[4])
     out.start()
     half = o_ref.shape[0]
     place = lax.broadcasted_iota(jnp.int32, (half, rows), 0) + (row * 2 + 1 - side) * half
     row_map = map_ref[pl.ds(leaf, 1), pl.ds(pl.multiple_of(row * rows, B), rows)]
     onehot = (place == row_map).astype(F32).astype(BF16)
-    o_ref[...] = pick_rows(onehot, split3(schur))
-    sent = pltpu.make_async_copy(o_ref, send_ref, sems.at[2])
+    o_ref[...] = pick_rows(onehot, split3(t_ref[...]))
+    sent = pltpu.make_async_copy(o_ref, send_ref, sems.at[5])
     sent.start()
     out.wait()
     sent.wait()
 
 
-def widen(value, maps, first, base):
+def widen(value, maps, first, base, split):
     blocks = len(maps)
     width = value.shape[1] // blocks
     total = first.shape[1]
@@ -348,7 +404,7 @@
         hi = -((-(b + 1) * step) // B) * B
         place = lax.broadcasted_iota(jnp.int32, (hi - lo, width), 0) + (lo + base)
         onehot = (place == maps[b]).astype(F32).astype(BF16)
-        first[:, lo:hi] = first[:, lo:hi] + pick_cols(split3(value[:, b * width : (b + 1) * width]), onehot)
+        first[:, lo:hi] = first[:, lo:hi] + pick_cols(split(value[:, b * width : (b + 1) * width]), onehot)
 
 
 def col_maps(map_ref, leaf, col, rows, cols):
@@ -368,14 +424,14 @@
     row_map = map_ref[pl.ds(leaf, 1), pl.ds(pl.multiple_of(row * rows, B), rows)]
     onehot = (place == row_map).astype(F32).astype(BF16)
     maps = col_maps(map_ref, leaf, col, rows, cols)
-    widen(pick_rows(onehot, split3(schur_ref[...])), maps, o_ref, col * total)
+    widen(pick_rows(onehot, split3(schur_ref[...])), maps, o_ref, col * total, split3)
 
 
 def add_kernel(rows, idx_ref, got_ref, map_ref, base_ref, o_ref):
     side, leaf, col = idx_ref[3], idx_ref[5], idx_ref[1]
     o_ref[...] = base_ref[...]
     maps = col_maps(map_ref, leaf + 1 - 2 * side, col, rows, got_ref.shape[1])
-    widen(got_ref[...], maps, o_ref, col * o_ref.shape[1])
+    widen(got_ref[...], maps, o_ref, col * o_ref.shape[1], split2)
 
 
 def on_device(pivot, border, update, child_map, parent_diag):
@@ -407,13 +463,13 @@
     bord, mine = lax.optimization_barrier((border[0], mine))
     turned = lax.ppermute(bord, ("row", "col"), turn)
     other = lax.ppermute(mine, "row", swap)
+    own = [lax.ppermute(bord, "col", [(y, (y + d) % ncol) for y in range(ncol)]) for d in range(1, ncol)]
 
     def factor(kernel, order, count, operands, specs, work):
         left = order - 2 * B * count
-        square = lambda m: jax.ShapeDtypeStruct((m, m), F32)
-        shapes = [square(left)] if left else []
+        shapes = [jax.ShapeDtypeStruct((2 * B * count, order), F32)]
         if left:
-            shapes = [jax.ShapeDtypeStruct((2 * B * count, order), F32)] + shapes
+            shapes.append(jax.ShapeDtypeStruct((left, left), F32))
         shapes += [
             jax.ShapeDtypeStruct((count, 2 * B, 2 * B), F32),
             jax.ShapeDtypeStruct((piece_rows, piece_cols), F32),
@@ -432,46 +488,63 @@
             **params(work, 58),
         )(idx, *operands)
 
-    top0, rest, inv0, block = factor(chol_first, n, 1, (mine, other), [VMEM, VMEM], 10**10)
-
-    bord, turned, inv0 = lax.optimization_barrier((bord, turned, inv0))
+    early = n // (4 * B)
+    late = n // (2 * B) - early
+    top0, rest, inv0, block = factor(chol_first, n, early, (mine, other), [VMEM, VMEM], 2 * 10**10)
+
+    turned, rest, *own = lax.optimization_barrier((turned, rest, *own))
     same = [[2 * x + c for x in range(nx)] for c in range(2)]
     col_mine = lax.all_to_all(
         jnp.broadcast_to(turned, (nx, rows, width)), "row", 0, 0, axis_index_groups=same, tiled=True
     )
-
-    middle = n // (2 * B) - 2
-    top1, rest, inv1, block = factor(
-        functools.partial(chol_next, 1), n - 2 * B, middle, (rest, block), [HBM, VMEM], 2 * 10**10
+    top1, inv1, pivot_out = factor(
+        functools.partial(chol_next, early), 2 * B * late, late, (rest, block), [HBM, VMEM], 2 * 10**10
     )
-    col_mine, rest, bord = lax.optimization_barrier((col_mine, rest, bord))
+
+    col_mine, inv1 = lax.optimization_barrier((col_mine, inv1))
     col_other = lax.ppermute(col_mine, "row", swap)
-    own = lax.all_to_all(jnp.broadcast_to(bord, (ncol, rows, width)), "col", 0, 0, tiled=True)
-    inv2, pivot_out = factor(functools.partial(chol_next, 1 + middle), 2 * B, 1, (rest, block), [HBM, VMEM], 10**10)
-
-    border_out, schur, send = pl.pallas_call(
-        solve_kernel,
+    half_f = jax.ShapeDtypeStruct((rows, n), BF16)
+    factor_refs = [pltpu.VMEM(top0.shape, F32), pltpu.VMEM(top1.shape, F32), pltpu.VMEM((ncol, 2 * B, 2 * B), F32)]
+    border_out, own_high, own_low, part = pl.pallas_call(
+        solve_first,
         out_shape=(
             jax.ShapeDtypeStruct((rows, width), F32),
+            half_f,
+            half_f,
+            jax.ShapeDtypeStruct((rows, rows), F32),
+        ),
+        in_specs=[SMEM] + [HBM] * 10,
+        out_specs=(VMEM, HBM, HBM, HBM),
+        scratch_shapes=[pltpu.VMEM((2 * rows, n), F32)]
+        + factor_refs
+        + [
+            pltpu.VMEM((2 * rows, n), BF16),
+            pltpu.VMEM((2 * rows, n), BF16),
+            pltpu.VMEM((rows, rows), F32),
+            pltpu.SemaphoreType.DMA((ncol, 4)),
+            pltpu.SemaphoreType.DMA((4,)),
+        ],
+        **params(10**10),
+    )(idx, bord, *own, col_mine, top0, top1, inv0, inv1, update[0])
+    schur, send = pl.pallas_call(
+        solve_last,
+        out_shape=(
             jax.ShapeDtypeStruct((rows, upd_cols), F32),
             jax.ShapeDtypeStruct((half, upd_cols), F32),
         ),
         in_specs=[SMEM] + [HBM] * 9 + [VMEM],
-        out_specs=(VMEM, HBM, HBM),
-        scratch_shapes=[
-            pltpu.VMEM((3 * rows, n), F32),
-            pltpu.VMEM(top0.shape, F32),
-            pltpu.VMEM(top1.shape, F32),
-            pltpu.VMEM((ncol, 2 * B, 2 * B), F32),
-            pltpu.VMEM((3 * rows, n), BF16),
-            pltpu.VMEM((3 * rows, n), BF16),
+        out_specs=(HBM, HBM),
+        scratch_shapes=[pltpu.VMEM((rows, n), F32)]
+        + factor_refs
+        + [pltpu.VMEM((rows, n), BF16)] * 4
+        + [
             pltpu.VMEM((rows, upd_cols), F32),
             pltpu.VMEM((half, upd_cols), F32),
-            pltpu.SemaphoreType.DMA((ncol, 5)),
-            pltpu.SemaphoreType.DMA((3,)),
+            pltpu.SemaphoreType.DMA((ncol, 3)),
+            pltpu.SemaphoreType.DMA((6,)),
         ],
         **params(10**10),
-    )(idx, own, col_mine, col_other, top0, top1, inv0, inv1, inv2, update[0], child_map)
+    )(idx, col_other, own_high, own_low, part, top0, top1, inv0, inv1, update[0], child_map)
 
     got = lax.ppermute(send, "leaf", [(s, s ^ 1) for s in range(lax.axis_size("leaf"))])
     base = pl.pallas_call(

time: 158 us -> 154 us (0.975)
  waiting for transfers between devices: 26.5 us -> 15.9 us
  starting transfers between devices: 24.4 us -> 31.5 us
    all_to_all x1 -> x0, waiting for transfers between devices: 9.37 us -> none  [on_device(): lax.all_to_all(jnp.broadcast_to(bord, (ncol, rows, width)), 'col', 0, 0,...]
    ppermute x0 -> x3, starting transfers between devices: none -> 8.53 us  [on_device(): lax.ppermute(bord, 'col', [(y, (y + d) % ncol) for y in range(ncol)])]
    pallas_call x1 -> x2, Pallas kernels: 16.3 us -> 22 us  [the longest x1 12.3 us: on_device(): pl.pallas_call(solve_first, out_shape=(jax.ShapeDtypeStruct((rows, width)...]
    pallas_call x3 -> x2, Pallas kernels: 52.1 us -> 47.8 us  [factor(): pl.pallas_call(kernel, out_shape=tuple(shapes), in_specs=[SMEM] + specs,...]
    all_to_all x1 -> x0, starting transfers between devices: 3.56 us -> none  [on_device(): lax.all_to_all(jnp.broadcast_to(bord, (ncol, rows, width)), 'col', 0, 0,...]
    ppermute x1, waiting for transfers between devices: 2.26 us -> 0.01 us  [on_device(): turned = lax.ppermute(bord, ('row', 'col'), turn)]
    all_to_all x1, starting transfers between devices: 3.94 us -> 5.86 us  [on_device(): lax.all_to_all(jnp.broadcast_to(turned, (nx, rows, width)), 'row', 0, 0,...]
    unnamed x18 -> x24, local copies, waits for them, and re-layouts: 3.54 us -> 3.54 us
  transfers between devices with their start and end apart: 6 -> 8, of which waited for: 3 -> 1; matrix products, arithmetic and copies ran while one was open for 1% -> 0% of each run, Pallas kernels for 35% -> 41%
where the time goes in v4:
time: 154 us; the launch traced here: 152 us
  Pallas kernels  77.7 us (50%)
  starting transfers between devices  31.5 us (20%)
  blocking collectives  20.7 us (13%)
  waiting for transfers between devices  15.9 us (10%)
  local copies, waits for them, and re-layouts  5.76 us (4%)
    pallas_call x2, Pallas kernels, factor(): pl.pallas_call(kernel, out_shape=tuple(shapes), in_specs=[SMEM] + specs,...  47.8 us
    all_to_all x1, blocking collectives, on_device(): lax.all_to_all(packed, ('row', 'col'), 0, 0, axis_index_groups=groups, ti...  20.7 us
    ppermute x1, waiting for transfers between devices, on_device(): lax.ppermute(send, 'leaf', [(s, s ^ 1) for s in range(lax.axis_size('leaf...  15.9 us
    pallas_call x1, Pallas kernels, on_device(): pl.pallas_call(solve_first, out_shape=(jax.ShapeDtypeStruct((rows, width)...  12.3 us
    pallas_call x1, Pallas kernels, on_device(): pl.pallas_call(solve_last, out_shape=(jax.ShapeDtypeStruct((rows, upd_col...  9.75 us
    ppermute x3, starting transfers between devices, on_device(): lax.ppermute(bord, 'col', [(y, (y + d) % ncol) for y in range(ncol)])  8.53 us
    all_to_all x1, starting transfers between devices, on_device(): lax.all_to_all(jnp.broadcast_to(turned, (nx, rows, width)), 'row', 0, 0,...  5.86 us
    ppermute x1, starting transfers between devices, on_device(): other = lax.ppermute(mine, 'row', swap)  5.77 us
  transfers between devices with their start and end apart: 8, of which 1 were waited for; matrix products, arithmetic and copies ran while one was open for 0% of the time, Pallas kernels for 41%

profile of v4, /device:TPU:7, one launch (start us, length us, event | category | flops | bytes accessed | tf_op | source)
XLA Modules:
  0.0 152.5 jit_solution(15080802141112373446)
XLA Ops:
  0.6 0.6 stack.23.idx_ref
  1.3 2.3 %shard_map.76 = f32[16,144,128]{2,1,0:T(8,128)} custom-call(s32[6]{0:T(128)} %stack.23.idx_ref, f32[128,256]{1,0:T(8,128)} %bitcast.12), custom_call_target="tpu_custom_call" | custom-call | flops 1000000 | bytes 8388608 | tf_op jit(solution)/shard_map/pallas_call | solution.py:451
  3.5 20.7 %all_to_all.10.mine_ref = f32[16,144,128]{2,1,0:T(8,128)S(1)} all-to-all(f32[16,144,128]{2,1,0:T(8,128)} %shard_map.76), channel_id=1, replica_groups={{0,1,2,3,8,9,10,11,16,17,18,19,24,25,26,27},{4,5,6,7,12,13,14,15,20,21,..., dimensions={0} | all-to-all | bytes 2359296 | tf_op jit(solution)/shard_map/all_to_all | solution.py:459
  24.3 5.8 %collective-permute-start.1 = (f32[16,144,128]{2,1,0:T(8,128)S(1)}, f32[16,144,128]{2,1,0:T(8,128)S(1)}, u32[]{:S(2)}, u32[]{:S(2)}) collective-permute-start(f32[16,144,128]{2,1,0:T(8,128)S(1)} %all_to_all.10.mine_ref), channel_id=1, source_target_pairs={{0,4},{4,0},{8,12},{12,8},{16,20},{20,16},{24,28},{28,24},{1,5},{5... | collective-permute-start | bytes 3538952 | tf_op jit(solution)/shard_map/ppermute | solution.py:465
  30.1 4.4 %collective-permute-start = (f32[384,256]{1,0:T(8,128)S(1)}, f32[384,256]{1,0:T(8,128)S(1)}, u32[]{:S(2)}, u32[]{:S(2)}) collective-permute-start(f32[384,256]{1,0:T(8,128)S(1)} %bitcast.17), channel_id=1, source_target_pairs={{0,0},{1,8},{2,16},{3,24},{4,4},{5,12},{6,20},{7,28},{8,1},{9,9},{... | collective-permute-start | bytes 1179656 | tf_op jit(solution)/shard_map/ppermute | solution.py:464
  34.5 2.3 %collective-permute-start.2 = (f32[384,256]{1,0:T(8,128)S(1)}, f32[384,256]{1,0:T(8,128)S(1)}, u32[]{:S(2)}, u32[]{:S(2)}) collective-permute-start(f32[384,256]{1,0:T(8,128)S(1)} %bitcast.18), channel_id=1, source_target_pairs={{0,1},{1,2},{2,3},{3,0},{4,5},{5,6},{6,7},{7,4},{8,9},{9,10},{10,1... | collective-permute-start | bytes 1179656 | tf_op jit(solution)/shard_map/ppermute | solution.py:466
  36.8 1.9 %collective-permute-start.3 = (f32[384,256]{1,0:T(8,128)S(1)}, f32[384,256]{1,0:T(8,128)S(1)}, u32[]{:S(2)}, u32[]{:S(2)}) collective-permute-start(f32[384,256]{1,0:T(8,128)S(1)} %bitcast.19), channel_id=1, source_target_pairs={{0,2},{1,3},{2,0},{3,1},{4,6},{5,7},{6,4},{7,5},{8,10},{9,11},{10,... | collective-permute-start | bytes 1179656 | tf_op jit(solution)/shard_map/ppermute | solution.py:466
  38.7 4.3 %collective-permute-start.4 = (f32[384,256]{1,0:T(8,128)S(1)}, f32[384,256]{1,0:T(8,128)S(1)}, u32[]{:S(2)}, u32[]{:S(2)}) collective-permute-start(f32[384,256]{1,0:T(8,128)S(1)} %bitcast.20), channel_id=1, source_target_pairs={{0,3},{1,0},{2,1},{3,2},{4,7},{5,4},{6,5},{7,6},{8,11},{9,8},{10,9... | collective-permute-start | bytes 1179656 | tf_op jit(solution)/shard_map/ppermute | solution.py:466
  43.0 0.0 collective-permute-done.1.other_ref
  43.0 1.0 copy-done.7
  44.1 26.7 %shard_map.77 = (f32[512,1024]{1,0:T(8,128)}, f32[512,512]{1,0:T(8,128)}, f32[2,256,256]{2,1,0:T(8,128)}, f32[128,256]{1,0:T(8,128)}) custom-call(s32[6]{0:T(128)} %stack.23.idx_ref, f32[16,144,128]{2,1,0:T(8,128)} %copy-done.4, f32[16,144,128]{2,1,0:T(8,128)} %copy-done.7), custom_call_target="tpu_custom_call" | custom-call | flops 20000000000 | bytes 8388608 | tf_op jit(solution)/shard_map/pallas_call | solution.py:477
  70.8 0.0 collective-permute-done
  70.8 0.0 collective-permute-done.2.own1_ref
  70.8 0.0 copy-start.9
  70.8 0.0 collective-permute-done.3.own2_ref
  70.8 0.0 collective-permute-done.4.own3_ref
  70.8 1.5 broadcast_in_dim.13
  72.3 5.9 %all-to-all-start.1 = ((f32[4,384,256]{2,1,0:T(8,128)}), f32[4,384,256]{2,1,0:T(8,128)S(1)}, u32[]{:S(2)}, u32[]{:S(2)}) async-start(f32[4,384,256]{2,1,0:T(8,128)} %broadcast_in_dim.13), calls=%async_computation.1 | async-start | bytes 3145728 | tf_op jit(solution)/shard_map/all_to_all | solution.py:497
  78.2 21.1 %shard_map.78 = (f32[512,512]{1,0:T(8,128)}, f32[2,256,256]{2,1,0:T(8,128)}, f32[128,256]{1,0:T(8,128)}) custom-call(s32[6]{0:T(128)} %stack.23.idx_ref, f32[512,512]{1,0:T(8,128)} %get-tuple-element.28.from_ref, f32[128,256]{1,0:T(8,128)} %get-tuple-element.29.before_ref), custom_call_target="tpu_custom_call" | custom-call | flops 20000000000 | bytes 8388608 | tf_op jit(solution)/shard_map/pallas_call | solution.py:477
  99.3 0.0 all-to-all-done.1.mine_ref
  99.3 3.3 %collective-permute-start.5 = (f32[4,384,256]{2,1,0:T(8,128)S(1)}, f32[4,384,256]{2,1,0:T(8,128)S(1)}, u32[]{:S(2)}, u32[]{:S(2)}) collective-permute-start(f32[4,384,256]{2,1,0:T(8,128)S(1)} %all-to-all-done.1.mine_ref), channel_id=1, source_target_pairs={{0,4},{4,0},{8,12},{12,8},{16,20},{20,16},{24,28},{28,24},{1,5},{5... | collective-permute-start | bytes 4718600 | tf_op jit(solution)/shard_map/ppermute | solution.py:505
  102.6 12.3 %shard_map.79 = (f32[384,256]{1,0:T(8,128)}, bf16[384,1024]{1,0:T(8,128)(2,1)}, bf16[384,1024]{1,0:T(8,128)(2,1)}, f32[384,384]{1,0:T(8,128)}) custom-call(s32[6]{0:T(128)} %stack.23.idx_ref, f32[384,256]{1,0:T(8,128)} %bitcast.16, f32[384,256]{1,0:T(8,128)} %copy-done.9, f32[384,256]{1,0:T(8,128)} %copy-done.10, f32[384,256]{1,0:T(8,128)} %copy-done.11, ...), custom_call_target="tpu_custom_call" | custom-call | flops 10000000000 | bytes 8388608 | tf_op jit(solution)/shard_map/pallas_call | solution.py:508
  114.9 0.0 collective-permute-done.5.other_ref
  114.9 1.2 copy-done.6
  116.2 9.8 %shard_map.80 = (f32[384,768]{1,0:T(8,128)}, f32[288,768]{1,0:T(8,128)}) custom-call(s32[6]{0:T(128)} %stack.23.idx_ref, f32[4,384,256]{2,1,0:T(8,128)} %copy-done.6, bf16[384,1024]{1,0:T(8,128)(2,1)} %get-tuple-element.42.oh_ref, bf16[384,1024]{1,0:T(8,128)(2,1)} %get-tuple-element.43.ol_ref, f32[384,384]{1,0:T(8,128)} %get-tuple-element.44.part_ref, ...), custom_call_target="tpu_custom_call" | custom-call | flops 10000000000 | bytes 8388608 | tf_op jit(solution)/shard_map/pallas_call | solution.py:529
  125.9 3.6 %collective-permute-start.6 = (f32[288,768]{1,0:T(8,128)}, f32[288,768]{1,0:T(8,128)S(1)}, u32[]{:S(2)}, u32[]{:S(2)}) collective-permute-start(f32[288,768]{1,0:T(8,128)} %get-tuple-element.45), channel_id=1, source_target_pairs={{0,32},{32,0},{64,96},{96,64},{128,160},{160,128},{192,224},{224,1... | collective-permute-start | bytes 2654216 | tf_op jit(solution)/shard_map/ppermute | solution.py:549
  129.6 0.1 copy.8.diag_ref
  129.7 0.0 copy-start.2
  129.7 1.3 copy-done.2
  131.0 2.9 %shard_map.81.base_ref = f32[288,1152]{1,0:T(8,128)S(1)} custom-call(s32[6]{0:T(128)S(1)} %copy-done, f32[384,768]{1,0:T(8,128)S(1)} %copy-done.2, s32[16,3072]{1,0:T(8,128)S(1)} %copy-done.1, f32[288,1]{1,0:T(8,128)S(1)} %copy.8.diag_ref), custom_call_target="tpu_custom_call" | custom-call | flops 2000000000 | bytes 8388608 | tf_op jit(solution)/shard_map/pallas_call | solution.py:550
  133.9 15.9 %collective-permute-done.6.got_ref = f32[288,768]{1,0:T(8,128)S(1)} collective-permute-done((f32[288,768]{1,0:T(8,128)}, f32[288,768]{1,0:T(8,128)S(1)}, u32[]{:S(2)}, u32[]{:S(2)}) %collective-permute-start.6) | collective-permute-done | bytes 884768 | tf_op jit(solution)/shard_map/ppermute | solution.py:549
  149.8 2.7 %shard_map.82 = f32[288,1152]{1,0:T(8,128)} custom-call(s32[6]{0:T(128)S(1)} %copy-done, f32[288,768]{1,0:T(8,128)S(1)} %collective-permute-done.6.got_ref, s32[16,3072]{1,0:T(8,128)S(1)} %copy-done.1, f32[288,1152]{1,0:T(8,128)S(1)} %shard_map.81.base_ref), custom_call_target="tpu_custom_call" | custom-call | flops 2000000000 | bytes 8388608 | tf_op jit(solution)/shard_map/pallas_call | solution.py:557
  (19 shorter events, 0.0 us)
Async XLA Ops:
  3.5 26.5 %copy-start.8 = (f32[1,384,256]{2,1,0:T(8,128)S(1)}, f32[1,384,256]{2,1,0:T(8,128)}, u32[]{:S(2)}) copy-start(f32[1,384,256]{2,1,0:T(8,128)} %param.6) | copy-start | bytes 1179652
  24.3 18.8 %copy-start.4 = (f32[16,144,128]{2,1,0:T(8,128)}, f32[16,144,128]{2,1,0:T(8,128)S(1)}, u32[]{:S(2)}) copy-start(f32[16,144,128]{2,1,0:T(8,128)S(1)} %all_to_all.10.mine_ref) | copy-start | bytes 3538948
  24.3 18.7 %collective-permute-start.1 = (f32[16,144,128]{2,1,0:T(8,128)S(1)}, f32[16,144,128]{2,1,0:T(8,128)S(1)}, u32[]{:S(2)}, u32[]{:S(2)}) collective-permute-start(f32[16,144,128]{2,1,0:T(8,128)S(1)} %all_to_all.10.mine_ref), channel_id=1, source_target_pairs={{0,4},{4,0},{8,12},{12,8},{16,20},{20,16},{24,28},{28,24},{1,5},{5... | collective-permute-start | bytes 3538952 | tf_op jit(solution)/shard_map/ppermute | solution.py:465
  30.1 40.7 %collective-permute-start = (f32[384,256]{1,0:T(8,128)S(1)}, f32[384,256]{1,0:T(8,128)S(1)}, u32[]{:S(2)}, u32[]{:S(2)}) collective-permute-start(f32[384,256]{1,0:T(8,128)S(1)} %bitcast.17), channel_id=1, source_target_pairs={{0,0},{1,8},{2,16},{3,24},{4,4},{5,12},{6,20},{7,28},{8,1},{9,9},{... | collective-permute-start | bytes 1179656 | tf_op jit(solution)/shard_map/ppermute | solution.py:464
  34.5 36.3 %collective-permute-start.2 = (f32[384,256]{1,0:T(8,128)S(1)}, f32[384,256]{1,0:T(8,128)S(1)}, u32[]{:S(2)}, u32[]{:S(2)}) collective-permute-start(f32[384,256]{1,0:T(8,128)S(1)} %bitcast.18), channel_id=1, source_target_pairs={{0,1},{1,2},{2,3},{3,0},{4,5},{5,6},{6,7},{7,4},{8,9},{9,10},{10,1... | collective-permute-start | bytes 1179656 | tf_op jit(solution)/shard_map/ppermute | solution.py:466
  36.8 34.0 %collective-permute-start.3 = (f32[384,256]{1,0:T(8,128)S(1)}, f32[384,256]{1,0:T(8,128)S(1)}, u32[]{:S(2)}, u32[]{:S(2)}) collective-permute-start(f32[384,256]{1,0:T(8,128)S(1)} %bitcast.19), channel_id=1, source_target_pairs={{0,2},{1,3},{2,0},{3,1},{4,6},{5,7},{6,4},{7,5},{8,10},{9,11},{10,... | collective-permute-start | bytes 1179656 | tf_op jit(solution)/shard_map/ppermute | solution.py:466
  38.7 32.1 %collective-permute-start.4 = (f32[384,256]{1,0:T(8,128)S(1)}, f32[384,256]{1,0:T(8,128)S(1)}, u32[]{:S(2)}, u32[]{:S(2)}) collective-permute-start(f32[384,256]{1,0:T(8,128)S(1)} %bitcast.20), channel_id=1, source_target_pairs={{0,3},{1,0},{2,1},{3,2},{4,7},{5,4},{6,5},{7,6},{8,11},{9,8},{10,9... | collective-permute-start | bytes 1179656 | tf_op jit(solution)/shard_map/ppermute | solution.py:466
  43.0 1.0 copy-start.7
  70.8 1.5 %copy-start.9 = (f32[384,256]{1,0:T(8,128)}, f32[384,256]{1,0:T(8,128)S(1)}, u32[]{:S(2)}) copy-start(f32[384,256]{1,0:T(8,128)S(1)} %collective-permute-done.2.own1_ref) | copy-start | bytes 1179652
  70.8 1.5 copy-start.10
  70.8 1.5 copy-start.11
  72.3 27.0 %all-to-all-start.1 = ((f32[4,384,256]{2,1,0:T(8,128)}), f32[4,384,256]{2,1,0:T(8,128)S(1)}, u32[]{:S(2)}, u32[]{:S(2)}) async-start(f32[4,384,256]{2,1,0:T(8,128)} %broadcast_in_dim.13), calls=%async_computation.1 | async-start | bytes 3145728 | tf_op jit(solution)/shard_map/all_to_all | solution.py:497
  99.3 3.3 %copy-start.3 = (f32[4,384,256]{2,1,0:T(8,128)}, f32[4,384,256]{2,1,0:T(8,128)S(1)}, u32[]{:S(2)}) copy-start(f32[4,384,256]{2,1,0:T(8,128)S(1)} %all-to-all-done.1.mine_ref) | copy-start | bytes 4718596
  99.3 15.6 %collective-permute-start.5 = (f32[4,384,256]{2,1,0:T(8,128)S(1)}, f32[4,384,256]{2,1,0:T(8,128)S(1)}, u32[]{:S(2)}, u32[]{:S(2)}) collective-permute-start(f32[4,384,256]{2,1,0:T(8,128)S(1)} %all-to-all-done.1.mine_ref), channel_id=1, source_target_pairs={{0,4},{4,0},{8,12},{12,8},{16,20},{20,16},{24,28},{28,24},{1,5},{5... | collective-permute-start | bytes 4718600 | tf_op jit(solution)/shard_map/ppermute | solution.py:505
  114.9 1.2 copy-start.6
  116.2 13.4 %copy-start.5 = (f32[1,288]{1,0:T(1,128)S(1)}, f32[1,288]{1,0:T(1,128)}, u32[]{:S(2)}) copy-start(f32[1,288]{1,0:T(1,128)} %param.9) | copy-start | bytes 3460
  116.2 13.6 %copy-start = (s32[6]{0:T(128)S(1)}, s32[6]{0:T(128)}, u32[]{:S(2)}) copy-start(s32[6]{0:T(128)} %stack.23.idx_ref) | copy-start | bytes 76
  116.2 13.6 %copy-start.1 = (s32[16,3072]{1,0:T(8,128)S(1)}, s32[16,3072]{1,0:T(8,128)}, u32[]{:S(2)}) copy-start(s32[16,3072]{1,0:T(8,128)} %map_ref.5) | copy-start | bytes 589828
  125.9 23.8 %collective-permute-start.6 = (f32[288,768]{1,0:T(8,128)}, f32[288,768]{1,0:T(8,128)S(1)}, u32[]{:S(2)}, u32[]{:S(2)}) collective-permute-start(f32[288,768]{1,0:T(8,128)} %get-tuple-element.45), channel_id=1, source_target_pairs={{0,32},{32,0},{64,96},{96,64},{128,160},{160,128},{192,224},{224,1... | collective-permute-start | bytes 2654216 | tf_op jit(solution)/shard_map/ppermute | solution.py:549
  129.7 1.3 copy-start.2

commit v5 on v3

--- a/solution.py
+++ b/solution.py
@@ -215,14 +215,10 @@
 
 
 def chol_next(first_col, idx_ref, from_ref, before_ref, *refs):
-    if len(refs) == 8:
-        top_ref, rest_ref, w_ref, l_ref, u_ref, v_ref, s_ref, sems = refs
-    else:
-        w_ref, l_ref, u_ref, v_ref, s_ref, sems = refs
-        top_ref = rest_ref = None
+    top_ref, w_ref, l_ref, u_ref, v_ref, s_ref, sems = refs
     copy_all((from_ref,), (u_ref,), sems)[0].wait()
     l_ref[...] = before_ref[...]
-    chol_end(u_ref, v_ref, s_ref, sems, top_ref, rest_ref, w_ref, l_ref, idx_ref[0], idx_ref[1], first_col)
+    chol_end(u_ref, v_ref, s_ref, sems, top_ref, None, w_ref, l_ref, idx_ref[0], idx_ref[1], first_col)
 
 
 def chol_end(u_ref, v_ref, s_ref, sems, top_ref, rest_ref, w_ref, l_ref, row, col, first_col):
@@ -230,10 +226,10 @@
     done = count * 2 * B
     left = u_ref.shape[0] - done
     chol_steps(u_ref, v_ref, s_ref, count * 2)
-    sources, targets = (v_ref,), (w_ref,)
+    sources, targets = (v_ref, u_ref.at[pl.ds(0, done)]), (w_ref, top_ref)
     if left > 0:
-        sources += (u_ref.at[pl.ds(done, left), pl.ds(done, left)], u_ref.at[pl.ds(0, done)])
-        targets += (rest_ref, top_ref)
+        sources += (u_ref.at[pl.ds(done, left), pl.ds(done, left)],)
+        targets += (rest_ref,)
     copies = copy_all(sources, targets, sems)
     rows, cols = l_ref.shape
     if first_col == 0:
@@ -273,8 +269,8 @@
 
 
 def solve_kernel(
-    idx_ref, own_ref, mine_ref, other_ref, top0_ref, top1_ref,
-    w0_ref, w1_ref, w2_ref, upd_ref, map_ref,
+    idx_ref, own0_ref, own1_ref, own2_ref, own3_ref, mine_ref, other_ref, top0_ref, top1_ref,
+    w0_ref, w1_ref, upd_ref, map_ref,
     fb_ref, schur_ref, send_ref,
     x_ref, u0_ref, u1_ref, v_ref, fh_ref, fl_ref, t_ref, o_ref, sem, sems,
 ):
@@ -283,12 +279,18 @@
 
     def load(y):
         cols = pl.ds(y * width, width)
-        found = [pltpu.make_async_copy(own_ref.at[y], x_ref.at[pl.ds(0, rows), cols], sem.at[y, 0])]
+        found = []
+        if y == 0:
+            for d, ref in enumerate((own0_ref, own1_ref, own2_ref, own3_ref)):
+                whose = lax.rem(col + ncol - d, ncol)
+                target = pl.ds(pl.multiple_of(whose * width, B), width)
+                found.append(pltpu.make_async_copy(ref, x_ref.at[pl.ds(0, rows), target], sem.at[d, 0]))
         for c, ref in ((core, mine_ref), (1 - core, other_ref)):
             target = pl.ds(pl.multiple_of((1 + c) * rows, B), rows)
             which = 1 if ref is mine_ref else 2
             found.append(pltpu.make_async_copy(ref.at[y], x_ref.at[target, cols], sem.at[y, which]))
-        inverse = (w0_ref.at[0], w1_ref.at[0], w1_ref.at[1], w2_ref.at[0])[y]
+        early = w0_ref.shape[0]
+        inverse = w0_ref.at[y] if y < early else w1_ref.at[y - early]
         found.append(pltpu.make_async_copy(inverse, v_ref.at[y], sem.at[y, 3]))
         if y == 0:
             found.append(pltpu.make_async_copy(top0_ref, u0_ref, sem.at[y, 4]))
@@ -331,14 +333,14 @@
     place = lax.broadcasted_iota(jnp.int32, (half, rows), 0) + (row * 2 + 1 - side) * half
     row_map = map_ref[pl.ds(leaf, 1), pl.ds(pl.multiple_of(row * rows, B), rows)]
     onehot = (place == row_map).astype(F32).astype(BF16)
-    o_ref[...] = pick_rows(onehot, split3(schur))
+    o_ref[...] = pick_rows(onehot, split2(schur))
     sent = pltpu.make_async_copy(o_ref, send_ref, sems.at[2])
     sent.start()
     out.wait()
     sent.wait()
 
 
-def widen(value, maps, first, base):
+def widen(value, maps, first, base, split):
     blocks = len(maps)
     width = value.shape[1] // blocks
     total = first.shape[1]
@@ -348,7 +350,7 @@
         hi = -((-(b + 1) * step) // B) * B
         place = lax.broadcasted_iota(jnp.int32, (hi - lo, width), 0) + (lo + base)
         onehot = (place == maps[b]).astype(F32).astype(BF16)
-        first[:, lo:hi] = first[:, lo:hi] + pick_cols(split3(value[:, b * width : (b + 1) * width]), onehot)
+        first[:, lo:hi] = first[:, lo:hi] + pick_cols(split(value[:, b * width : (b + 1) * width]), onehot)
 
 
 def col_maps(map_ref, leaf, col, rows, cols):
@@ -368,14 +370,14 @@
     row_map = map_ref[pl.ds(leaf, 1), pl.ds(pl.multiple_of(row * rows, B), rows)]
     onehot = (place == row_map).astype(F32).astype(BF16)
     maps = col_maps(map_ref, leaf, col, rows, cols)
-    widen(pick_rows(onehot, split3(schur_ref[...])), maps, o_ref, col * total)
+    widen(pick_rows(onehot, split3(schur_ref[...])), maps, o_ref, col * total, split3)
 
 
 def add_kernel(rows, idx_ref, got_ref, map_ref, base_ref, o_ref):
     side, leaf, col = idx_ref[3], idx_ref[5], idx_ref[1]
     o_ref[...] = base_ref[...]
     maps = col_maps(map_ref, leaf + 1 - 2 * side, col, rows, got_ref.shape[1])
-    widen(got_ref[...], maps, o_ref, col * o_ref.shape[1])
+    widen(got_ref[...], maps, o_ref, col * o_ref.shape[1], split2)
 
 
 def on_device(pivot, border, update, child_map, parent_diag):
@@ -407,13 +409,13 @@
     bord, mine = lax.optimization_barrier((border[0], mine))
     turned = lax.ppermute(bord, ("row", "col"), turn)
     other = lax.ppermute(mine, "row", swap)
+    own = [lax.ppermute(bord, "col", [(y, (y + d) % ncol) for y in range(ncol)]) for d in range(1, ncol)]
 
     def factor(kernel, order, count, operands, specs, work):
         left = order - 2 * B * count
-        square = lambda m: jax.ShapeDtypeStruct((m, m), F32)
-        shapes = [square(left)] if left else []
+        shapes = [jax.ShapeDtypeStruct((2 * B * count, order), F32)]
         if left:
-            shapes = [jax.ShapeDtypeStruct((2 * B * count, order), F32)] + shapes
+            shapes.append(jax.ShapeDtypeStruct((left, left), F32))
         shapes += [
             jax.ShapeDtypeStruct((count, 2 * B, 2 * B), F32),
             jax.ShapeDtypeStruct((piece_rows, piece_cols), F32),
@@ -432,23 +434,21 @@
             **params(work, 58),
         )(idx, *operands)
 
-    top0, rest, inv0, block = factor(chol_first, n, 1, (mine, other), [VMEM, VMEM], 10**10)
-
-    bord, turned, inv0 = lax.optimization_barrier((bord, turned, inv0))
+    early = n // (4 * B)
+    late = n // (2 * B) - early
+    top0, rest, inv0, block = factor(chol_first, n, early, (mine, other), [VMEM, VMEM], 2 * 10**10)
+
+    turned, rest, *own = lax.optimization_barrier((turned, rest, *own))
     same = [[2 * x + c for x in range(nx)] for c in range(2)]
     col_mine = lax.all_to_all(
         jnp.broadcast_to(turned, (nx, rows, width)), "row", 0, 0, axis_index_groups=same, tiled=True
     )
-
-    middle = n // (2 * B) - 2
-    top1, rest, inv1, block = factor(
-        functools.partial(chol_next, 1), n - 2 * B, middle, (rest, block), [HBM, VMEM], 2 * 10**10
+    top1, inv1, pivot_out = factor(
+        functools.partial(chol_next, early), 2 * B * late, late, (rest, block), [HBM, VMEM], 2 * 10**10
     )
-    col_mine, rest, bord = lax.optimization_barrier((col_mine, rest, bord))
+
+    col_mine, inv1 = lax.optimization_barrier((col_mine, inv1))
     col_other = lax.ppermute(col_mine, "row", swap)
-    own = lax.all_to_all(jnp.broadcast_to(bord, (ncol, rows, width)), "col", 0, 0, tiled=True)
-    inv2, pivot_out = factor(functools.partial(chol_next, 1 + middle), 2 * B, 1, (rest, block), [HBM, VMEM], 10**10)
-
     border_out, schur, send = pl.pallas_call(
         solve_kernel,
         out_shape=(
@@ -456,7 +456,7 @@
             jax.ShapeDtypeStruct((rows, upd_cols), F32),
             jax.ShapeDtypeStruct((half, upd_cols), F32),
         ),
-        in_specs=[SMEM] + [HBM] * 9 + [VMEM],
+        in_specs=[SMEM] + [HBM] * 11 + [VMEM],
         out_specs=(VMEM, HBM, HBM),
         scratch_shapes=[
             pltpu.VMEM((3 * rows, n), F32),
@@ -470,8 +470,8 @@
             pltpu.SemaphoreType.DMA((ncol, 5)),
             pltpu.SemaphoreType.DMA((3,)),
         ],
-        **params(10**10),
-    )(idx, own, col_mine, col_other, top0, top1, inv0, inv1, inv2, update[0], child_map)
+        **params(10**10, 60),
+    )(idx, bord, *own, col_mine, col_other, top0, top1, inv0, inv1, update[0], child_map)
 
     got = lax.ppermute(send, "leaf", [(s, s ^ 1) for s in range(lax.axis_size("leaf"))])
     base = pl.pallas_call(

time: 158 us -> 152 us (0.962)
  waiting for transfers between devices: 26.5 us -> 18.6 us
  starting transfers between devices: 24.4 us -> 31.5 us
  Pallas kernels: 76.9 us -> 73.1 us
    all_to_all x1 -> x0, waiting for transfers between devices: 9.37 us -> none  [on_device(): lax.all_to_all(jnp.broadcast_to(bord, (ncol, rows, width)), 'col', 0, 0,...]
    ppermute x0 -> x3, starting transfers between devices: none -> 8.53 us  [on_device(): lax.ppermute(bord, 'col', [(y, (y + d) % ncol) for y in range(ncol)])]
    pallas_call x3 -> x2, Pallas kernels: 52.1 us -> 47.9 us  [factor(): pl.pallas_call(kernel, out_shape=tuple(shapes), in_specs=[SMEM] + specs,...]
    all_to_all x1 -> x0, starting transfers between devices: 3.56 us -> none  [on_device(): lax.all_to_all(jnp.broadcast_to(bord, (ncol, rows, width)), 'col', 0, 0,...]
    ppermute x1, waiting for transfers between devices: 0.01 us -> 3.01 us  [on_device(): col_other = lax.ppermute(col_mine, 'row', swap)]
    ppermute x1, waiting for transfers between devices: 2.26 us -> 0.01 us  [on_device(): turned = lax.ppermute(bord, ('row', 'col'), turn)]
    all_to_all x1, starting transfers between devices: 3.94 us -> 5.86 us  [on_device(): lax.all_to_all(jnp.broadcast_to(turned, (nx, rows, width)), 'row', 0, 0,...]
    unnamed x18 -> x24, local copies, waits for them, and re-layouts: 3.54 us -> 3.56 us
  transfers between devices with their start and end apart: 6 -> 8, of which waited for: 3 -> 2; matrix products, arithmetic and copies ran while one was open for 1% -> 0% of each run, Pallas kernels for 35% -> 34%
where the time goes in v5:
time: 152 us; the launch traced here: 151 us
  Pallas kernels  73.1 us (48%)
  starting transfers between devices  31.5 us (21%)
  blocking collectives  20.7 us (14%)
  waiting for transfers between devices  18.6 us (12%)
  local copies, waits for them, and re-layouts  5.79 us (4%)
    pallas_call x2, Pallas kernels, factor(): pl.pallas_call(kernel, out_shape=tuple(shapes), in_specs=[SMEM] + specs,...  47.9 us
    all_to_all x1, blocking collectives, on_device(): lax.all_to_all(packed, ('row', 'col'), 0, 0, axis_index_groups=groups, ti...  20.7 us
    pallas_call x1, Pallas kernels, on_device(): pl.pallas_call(solve_kernel, out_shape=(jax.ShapeDtypeStruct((rows, width...  17.3 us
    ppermute x1, waiting for transfers between devices, on_device(): lax.ppermute(send, 'leaf', [(s, s ^ 1) for s in range(lax.axis_size('leaf...  15.5 us
    ppermute x3, starting transfers between devices, on_device(): lax.ppermute(bord, 'col', [(y, (y + d) % ncol) for y in range(ncol)])  8.53 us
    all_to_all x1, starting transfers between devices, on_device(): lax.all_to_all(jnp.broadcast_to(turned, (nx, rows, width)), 'row', 0, 0,...  5.86 us
    ppermute x1, starting transfers between devices, on_device(): other = lax.ppermute(mine, 'row', swap)  5.77 us
    ppermute x1, starting transfers between devices, on_device(): turned = lax.ppermute(bord, ('row', 'col'), turn)  4.39 us
  transfers between devices with their start and end apart: 8, of which 2 were waited for; matrix products, arithmetic and copies ran while one was open for 0% of the time, Pallas kernels for 34%

profile of v5, /device:TPU:7, one launch (start us, length us, event | category | flops | bytes accessed | tf_op | source)
XLA Modules:
  0.0 150.6 jit_solution(2807306086587292878)
XLA Ops:
  0.6 0.6 stack.23.idx_ref
  1.3 2.3 %shard_map.76 = f32[16,144,128]{2,1,0:T(8,128)} custom-call(s32[6]{0:T(128)} %stack.23.idx_ref, f32[128,256]{1,0:T(8,128)} %bitcast.12), custom_call_target="tpu_custom_call" | custom-call | flops 1000000 | bytes 8388608 | tf_op jit(solution)/shard_map/pallas_call | solution.py:397
  3.6 20.7 %all_to_all.10.mine_ref = f32[16,144,128]{2,1,0:T(8,128)S(1)} all-to-all(f32[16,144,128]{2,1,0:T(8,128)} %shard_map.76), channel_id=1, replica_groups={{0,1,2,3,8,9,10,11,16,17,18,19,24,25,26,27},{4,5,6,7,12,13,14,15,20,21,..., dimensions={0} | all-to-all | bytes 2359296 | tf_op jit(solution)/shard_map/all_to_all | solution.py:405
  24.3 5.8 %collective-permute-start.1 = (f32[16,144,128]{2,1,0:T(8,128)S(1)}, f32[16,144,128]{2,1,0:T(8,128)S(1)}, u32[]{:S(2)}, u32[]{:S(2)}) collective-permute-start(f32[16,144,128]{2,1,0:T(8,128)S(1)} %all_to_all.10.mine_ref), channel_id=1, source_target_pairs={{0,4},{4,0},{8,12},{12,8},{16,20},{20,16},{24,28},{28,24},{1,5},{5... | collective-permute-start | bytes 3538952 | tf_op jit(solution)/shard_map/ppermute | solution.py:411
  30.1 4.4 %collective-permute-start = (f32[384,256]{1,0:T(8,128)S(1)}, f32[384,256]{1,0:T(8,128)S(1)}, u32[]{:S(2)}, u32[]{:S(2)}) collective-permute-start(f32[384,256]{1,0:T(8,128)S(1)} %bitcast.16), channel_id=1, source_target_pairs={{0,0},{1,8},{2,16},{3,24},{4,4},{5,12},{6,20},{7,28},{8,1},{9,9},{... | collective-permute-start | bytes 1179656 | tf_op jit(solution)/shard_map/ppermute | solution.py:410
  34.5 2.3 %collective-permute-start.2 = (f32[384,256]{1,0:T(8,128)S(1)}, f32[384,256]{1,0:T(8,128)S(1)}, u32[]{:S(2)}, u32[]{:S(2)}) collective-permute-start(f32[384,256]{1,0:T(8,128)S(1)} %bitcast.17), channel_id=1, source_target_pairs={{0,1},{1,2},{2,3},{3,0},{4,5},{5,6},{6,7},{7,4},{8,9},{9,10},{10,1... | collective-permute-start | bytes 1179656 | tf_op jit(solution)/shard_map/ppermute | solution.py:412
  36.8 1.9 %collective-permute-start.3 = (f32[384,256]{1,0:T(8,128)S(1)}, f32[384,256]{1,0:T(8,128)S(1)}, u32[]{:S(2)}, u32[]{:S(2)}) collective-permute-start(f32[384,256]{1,0:T(8,128)S(1)} %bitcast.18), channel_id=1, source_target_pairs={{0,2},{1,3},{2,0},{3,1},{4,6},{5,7},{6,4},{7,5},{8,10},{9,11},{10,... | collective-permute-start | bytes 1179656 | tf_op jit(solution)/shard_map/ppermute | solution.py:412
  38.7 4.3 %collective-permute-start.4 = (f32[384,256]{1,0:T(8,128)S(1)}, f32[384,256]{1,0:T(8,128)S(1)}, u32[]{:S(2)}, u32[]{:S(2)}) collective-permute-start(f32[384,256]{1,0:T(8,128)S(1)} %bitcast.19), channel_id=1, source_target_pairs={{0,3},{1,0},{2,1},{3,2},{4,7},{5,4},{6,5},{7,6},{8,11},{9,8},{10,9... | collective-permute-start | bytes 1179656 | tf_op jit(solution)/shard_map/ppermute | solution.py:412
  43.0 0.0 collective-permute-done.1.other_ref
  43.1 1.0 copy-done.7
  44.1 26.7 %shard_map.77 = (f32[512,1024]{1,0:T(8,128)}, f32[512,512]{1,0:T(8,128)}, f32[2,256,256]{2,1,0:T(8,128)}, f32[128,256]{1,0:T(8,128)}) custom-call(s32[6]{0:T(128)} %stack.23.idx_ref, f32[16,144,128]{2,1,0:T(8,128)} %copy-done.4, f32[16,144,128]{2,1,0:T(8,128)} %copy-done.7), custom_call_target="tpu_custom_call" | custom-call | flops 20000000000 | bytes 8388608 | tf_op jit(solution)/shard_map/pallas_call | solution.py:423
  70.8 0.0 collective-permute-done
  70.8 0.0 collective-permute-done.2.own1_ref
  70.9 0.0 collective-permute-done.3.own2_ref
  70.9 0.0 collective-permute-done.4.own3_ref
  70.9 1.5 broadcast_in_dim.13
  72.4 0.1 copy-done.11
  72.5 5.9 %all-to-all-start.1 = ((f32[4,384,256]{2,1,0:T(8,128)}), f32[4,384,256]{2,1,0:T(8,128)S(1)}, u32[]{:S(2)}, u32[]{:S(2)}) async-start(f32[4,384,256]{2,1,0:T(8,128)} %broadcast_in_dim.13), calls=%async_computation.1 | async-start | bytes 3145728 | tf_op jit(solution)/shard_map/all_to_all | solution.py:443
  78.3 21.1 %shard_map.78 = (f32[512,512]{1,0:T(8,128)}, f32[2,256,256]{2,1,0:T(8,128)}, f32[128,256]{1,0:T(8,128)}) custom-call(s32[6]{0:T(128)} %stack.23.idx_ref, f32[512,512]{1,0:T(8,128)} %get-tuple-element.25.from_ref, f32[128,256]{1,0:T(8,128)} %get-tuple-element.26.before_ref), custom_call_target="tpu_custom_call" | custom-call | flops 20000000000 | bytes 8388608 | tf_op jit(solution)/shard_map/pallas_call | solution.py:423
  99.5 0.0 all-to-all-done.1.mine_ref
  99.5 0.0 copy-start.3
  99.5 3.3 %collective-permute-start.5 = (f32[4,384,256]{2,1,0:T(8,128)S(1)}, f32[4,384,256]{2,1,0:T(8,128)S(1)}, u32[]{:S(2)}, u32[]{:S(2)}) collective-permute-start(f32[4,384,256]{2,1,0:T(8,128)S(1)} %all-to-all-done.1.mine_ref), channel_id=1, source_target_pairs={{0,4},{4,0},{8,12},{12,8},{16,20},{20,16},{24,28},{28,24},{1,5},{5... | collective-permute-start | bytes 4718600 | tf_op jit(solution)/shard_map/ppermute | solution.py:451
  102.8 3.0 %collective-permute-done.5.other_ref = f32[4,384,256]{2,1,0:T(8,128)S(1)} collective-permute-done((f32[4,384,256]{2,1,0:T(8,128)S(1)}, f32[4,384,256]{2,1,0:T(8,128)S(1)}, u32[]{:S(2)}, u32[]{:S(2)}) %collective-permute-start.5) | collective-permute-done | bytes 1572896 | tf_op jit(solution)/shard_map/ppermute | solution.py:451
  105.9 1.2 copy-done.6
  107.0 17.3 %shard_map.79 = (f32[384,256]{1,0:T(8,128)}, f32[384,768]{1,0:T(8,128)}, f32[288,768]{1,0:T(8,128)}) custom-call(s32[6]{0:T(128)} %stack.23.idx_ref, f32[384,256]{1,0:T(8,128)} %bitcast.15, f32[384,256]{1,0:T(8,128)} %copy-done.9, f32[384,256]{1,0:T(8,128)} %copy-done.10, f32[384,256]{1,0:T(8,128)} %copy-done.11, f32[4,384,256]{2,1,0:T(8,128)} %copy-done.3, ...), custom_call_target="tpu_custom_call" | custom-call | flops 10000000000 | bytes 8388608 | tf_op jit(solution)/shard_map/pallas_call | solution.py:452
  124.3 3.6 %collective-permute-start.6 = (f32[288,768]{1,0:T(8,128)}, f32[288,768]{1,0:T(8,128)S(1)}, u32[]{:S(2)}, u32[]{:S(2)}) collective-permute-start(f32[288,768]{1,0:T(8,128)} %get-tuple-element.39), channel_id=1, source_target_pairs={{0,32},{32,0},{64,96},{96,64},{128,160},{160,128},{192,224},{224,1... | collective-permute-start | bytes 2654216 | tf_op jit(solution)/shard_map/ppermute | solution.py:476
  128.0 0.1 copy.8.diag_ref
  128.1 0.0 copy-start.2
  128.1 1.3 copy-done.2
  129.4 2.9 %shard_map.80.base_ref = f32[288,1152]{1,0:T(8,128)S(1)} custom-call(s32[6]{0:T(128)S(1)} %copy-done, f32[384,768]{1,0:T(8,128)S(1)} %copy-done.2, s32[16,3072]{1,0:T(8,128)S(1)} %copy-done.1, f32[288,1]{1,0:T(8,128)S(1)} %copy.8.diag_ref), custom_call_target="tpu_custom_call" | custom-call | flops 2000000000 | bytes 8388608 | tf_op jit(solution)/shard_map/pallas_call | solution.py:477
  132.3 15.5 %collective-permute-done.6.got_ref = f32[288,768]{1,0:T(8,128)S(1)} collective-permute-done((f32[288,768]{1,0:T(8,128)}, f32[288,768]{1,0:T(8,128)S(1)}, u32[]{:S(2)}, u32[]{:S(2)}) %collective-permute-start.6) | collective-permute-done | bytes 884768 | tf_op jit(solution)/shard_map/ppermute | solution.py:476
  147.8 2.7 %shard_map.81 = f32[288,1152]{1,0:T(8,128)} custom-call(s32[6]{0:T(128)S(1)} %copy-done, f32[288,768]{1,0:T(8,128)S(1)} %collective-permute-done.6.got_ref, s32[16,3072]{1,0:T(8,128)S(1)} %copy-done.1, f32[288,1152]{1,0:T(8,128)S(1)} %shard_map.80.base_ref), custom_call_target="tpu_custom_call" | custom-call | flops 2000000000 | bytes 8388608 | tf_op jit(solution)/shard_map/pallas_call | solution.py:484
  (18 shorter events, 0.0 us)
Async XLA Ops:
  3.6 26.5 %copy-start.8 = (f32[1,384,256]{2,1,0:T(8,128)S(1)}, f32[1,384,256]{2,1,0:T(8,128)}, u32[]{:S(2)}) copy-start(f32[1,384,256]{2,1,0:T(8,128)} %param.6) | copy-start | bytes 1179652
  24.3 18.8 %copy-start.4 = (f32[16,144,128]{2,1,0:T(8,128)}, f32[16,144,128]{2,1,0:T(8,128)S(1)}, u32[]{:S(2)}) copy-start(f32[16,144,128]{2,1,0:T(8,128)S(1)} %all_to_all.10.mine_ref) | copy-start | bytes 3538948
  24.3 18.7 %collective-permute-start.1 = (f32[16,144,128]{2,1,0:T(8,128)S(1)}, f32[16,144,128]{2,1,0:T(8,128)S(1)}, u32[]{:S(2)}, u32[]{:S(2)}) collective-permute-start(f32[16,144,128]{2,1,0:T(8,128)S(1)} %all_to_all.10.mine_ref), channel_id=1, source_target_pairs={{0,4},{4,0},{8,12},{12,8},{16,20},{20,16},{24,28},{28,24},{1,5},{5... | collective-permute-start | bytes 3538952 | tf_op jit(solution)/shard_map/ppermute | solution.py:411
  30.1 40.8 %collective-permute-start = (f32[384,256]{1,0:T(8,128)S(1)}, f32[384,256]{1,0:T(8,128)S(1)}, u32[]{:S(2)}, u32[]{:S(2)}) collective-permute-start(f32[384,256]{1,0:T(8,128)S(1)} %bitcast.16), channel_id=1, source_target_pairs={{0,0},{1,8},{2,16},{3,24},{4,4},{5,12},{6,20},{7,28},{8,1},{9,9},{... | collective-permute-start | bytes 1179656 | tf_op jit(solution)/shard_map/ppermute | solution.py:410
  34.5 36.4 %collective-permute-start.2 = (f32[384,256]{1,0:T(8,128)S(1)}, f32[384,256]{1,0:T(8,128)S(1)}, u32[]{:S(2)}, u32[]{:S(2)}) collective-permute-start(f32[384,256]{1,0:T(8,128)S(1)} %bitcast.17), channel_id=1, source_target_pairs={{0,1},{1,2},{2,3},{3,0},{4,5},{5,6},{6,7},{7,4},{8,9},{9,10},{10,1... | collective-permute-start | bytes 1179656 | tf_op jit(solution)/shard_map/ppermute | solution.py:412
  36.8 34.1 %collective-permute-start.3 = (f32[384,256]{1,0:T(8,128)S(1)}, f32[384,256]{1,0:T(8,128)S(1)}, u32[]{:S(2)}, u32[]{:S(2)}) collective-permute-start(f32[384,256]{1,0:T(8,128)S(1)} %bitcast.18), channel_id=1, source_target_pairs={{0,2},{1,3},{2,0},{3,1},{4,6},{5,7},{6,4},{7,5},{8,10},{9,11},{10,... | collective-permute-start | bytes 1179656 | tf_op jit(solution)/shard_map/ppermute | solution.py:412
  38.7 32.2 %collective-permute-start.4 = (f32[384,256]{1,0:T(8,128)S(1)}, f32[384,256]{1,0:T(8,128)S(1)}, u32[]{:S(2)}, u32[]{:S(2)}) collective-permute-start(f32[384,256]{1,0:T(8,128)S(1)} %bitcast.19), channel_id=1, source_target_pairs={{0,3},{1,0},{2,1},{3,2},{4,7},{5,4},{6,5},{7,6},{8,11},{9,8},{10,9... | collective-permute-start | bytes 1179656 | tf_op jit(solution)/shard_map/ppermute | solution.py:412
  43.1 1.0 copy-start.7
  70.9 1.5 %copy-start.9 = (f32[384,256]{1,0:T(8,128)}, f32[384,256]{1,0:T(8,128)S(1)}, u32[]{:S(2)}) copy-start(f32[384,256]{1,0:T(8,128)S(1)} %collective-permute-done.2.own1_ref) | copy-start | bytes 1179652
  70.9 1.5 copy-start.10
  70.9 1.6 %copy-start.11 = (f32[384,256]{1,0:T(8,128)}, f32[384,256]{1,0:T(8,128)S(1)}, u32[]{:S(2)}) copy-start(f32[384,256]{1,0:T(8,128)S(1)} %collective-permute-done.4.own3_ref) | copy-start | bytes 1179652
  72.5 27.0 %all-to-all-start.1 = ((f32[4,384,256]{2,1,0:T(8,128)}), f32[4,384,256]{2,1,0:T(8,128)S(1)}, u32[]{:S(2)}, u32[]{:S(2)}) async-start(f32[4,384,256]{2,1,0:T(8,128)} %broadcast_in_dim.13), calls=%async_computation.1 | async-start | bytes 3145728 | tf_op jit(solution)/shard_map/all_to_all | solution.py:443
  99.5 6.4 %copy-start.3 = (f32[4,384,256]{2,1,0:T(8,128)}, f32[4,384,256]{2,1,0:T(8,128)S(1)}, u32[]{:S(2)}) copy-start(f32[4,384,256]{2,1,0:T(8,128)S(1)} %all-to-all-done.1.mine_ref) | copy-start | bytes 4718596
  99.5 6.4 %collective-permute-start.5 = (f32[4,384,256]{2,1,0:T(8,128)S(1)}, f32[4,384,256]{2,1,0:T(8,128)S(1)}, u32[]{:S(2)}, u32[]{:S(2)}) collective-permute-start(f32[4,384,256]{2,1,0:T(8,128)S(1)} %all-to-all-done.1.mine_ref), channel_id=1, source_target_pairs={{0,4},{4,0},{8,12},{12,8},{16,20},{20,16},{24,28},{28,24},{1,5},{5... | collective-permute-start | bytes 4718600 | tf_op jit(solution)/shard_map/ppermute | solution.py:451
  105.9 1.2 copy-start.6
  107.0 20.9 %copy-start.5 = (f32[1,288]{1,0:T(1,128)S(1)}, f32[1,288]{1,0:T(1,128)}, u32[]{:S(2)}) copy-start(f32[1,288]{1,0:T(1,128)} %param.9) | copy-start | bytes 3460
  107.0 21.1 %copy-start = (s32[6]{0:T(128)S(1)}, s32[6]{0:T(128)}, u32[]{:S(2)}) copy-start(s32[6]{0:T(128)} %stack.23.idx_ref) | copy-start | bytes 76
  107.0 21.1 %copy-start.1 = (s32[16,3072]{1,0:T(8,128)S(1)}, s32[16,3072]{1,0:T(8,128)}, u32[]{:S(2)}) copy-start(s32[16,3072]{1,0:T(8,128)} %map_ref.5) | copy-start | bytes 589828
  124.3 23.5 %collective-permute-start.6 = (f32[288,768]{1,0:T(8,128)}, f32[288,768]{1,0:T(8,128)S(1)}, u32[]{:S(2)}, u32[]{:S(2)}) collective-permute-start(f32[288,768]{1,0:T(8,128)} %get-tuple-element.39), channel_id=1, source_target_pairs={{0,32},{32,0},{64,96},{96,64},{128,160},{160,128},{192,224},{224,1... | collective-permute-start | bytes 2654216 | tf_op jit(solution)/shard_map/ppermute | solution.py:476
  128.1 1.3 copy-start.2
